TPU v7x, 32 devices: a whole 2x2x4 slice. The times are simulated.
32 devices in a mesh: src: 16 (over z, x, core), tgt: 2 (over y).
Axes of the slice: x: 2, y: 2, z: 4, core: 2. Of those that a mesh axis runs over, the one named last changes fastest.
Arguments:
- upstream: bfloat16 [128, 128, 324], P('src'), may hold values from -6 to 6
- centers: int32 [2, 128, 128], P(None, 'src'), may hold values from -4 to 259, as said below
- post_relu: bfloat16 [128, 128, 128], P('src'), as said below
- conv_input: bfloat16 [128, 128, 128], P(('src', 'tgt')), may hold values from -6 to 6
- target_feats: bfloat16 [16, 256, 256], P('tgt'), may hold values from -6 to 6
- out_weight: bfloat16 [128, 256], replicated, may hold values from -0.5 to 0.5
- conv_weight: bfloat16 [3, 3, 128, 128], replicated, may hold values from -0.1875 to 0.1875
Outputs:
- tgt_grad: bfloat16 [16, 256, 256], P('tgt', 'src')
- act_grad: bfloat16 [128, 128, 128], P(('src', 'tgt'))
- out_wgrad: float32 [128, 256], replicated
- conv_wgrad: float32 [3, 3, 128, 128], replicated
Inputs may be any that keep to these rules, and one draw needn't show every extreme that they name: centers[0] is a target row from -4 to 19 and centers[1] a target column from -4 to 259; windows may reach outside the target image. `post_relu`: entries are zero or positive.
All inputs are finite; a program needn't handle non-finite values.
Results may differ from a plain program's by a relative error of at most 0.0064.
Values may be sent and summed in bfloat16 or wider, within the bound.
A program may use at most 64 MiB of HBM per device.

v0:
```python
import math

import jax
import jax.numpy as jnp
from jax import lax
from jax.sharding import PartitionSpec as P


def padded_2(array, sides, width):
    for axis, dim in sides:
        devices, length = (lax.axis_size(axis), array.shape[dim])
        up = [(i, (i + 1) % devices) for i in range(devices - 1)]
        down = [(j, i) for i, j in up]
        last = lax.slice_in_dim(array, length - width, length, axis=dim)
        first = lax.slice_in_dim(array, 0, width, axis=dim)
        before = lax.ppermute(last, axis, up)
        after = lax.ppermute(first, axis, down)
        array = jnp.concatenate([before, array, after], axis=dim)
    return array


def corr_block(center_rows, center_cols, grad_rows, row_start, row_total, col_total):
    source_total = grad_rows.shape[0]
    row_ids = row_start + jnp.arange(row_total, dtype=jnp.int32)
    col_ids = jnp.arange(col_total, dtype=jnp.int32)
    offsets = jnp.arange(9, dtype=jnp.int32)
    row_parts = []
    col_parts = []
    for level_no in range(4):
        level_step = 2**level_no
        row_off = (
            jnp.floor_divide(row_ids, level_step)[None, :]
            - jnp.floor_divide(center_rows, level_step)[:, None]
            + 4
        )
        col_off = (
            jnp.floor_divide(col_ids, level_step)[None, :]
            - jnp.floor_divide(center_cols, level_step)[:, None]
            + 4
        )
        row_hot = jnp.where(
            row_off[:, None, :] == offsets[None, :, None], 0.25**level_no, 0.0
        ).astype(jnp.float32)
        col_hot = jnp.where(col_off[:, None, :] == offsets[None, :, None], 1.0, 0.0).astype(
            jnp.float32
        )
        level_grads = (
            grad_rows[:, 81 * level_no : 81 * (level_no + 1)]
            .astype(jnp.float32)
            .reshape(source_total, 9, 9)
        )
        row_parts.append(row_hot)
        col_parts.append(jnp.einsum("sab,sbx->sax", level_grads, col_hot))
    row_table = jnp.concatenate(row_parts, axis=1)
    col_table = jnp.concatenate(col_parts, axis=1)
    return jnp.einsum("say,sax->syx", row_table, col_table).astype(jnp.bfloat16)


def hidden_grads(src_grad, relu_rows, out_weight):
    hidden = jnp.einsum("rwd,cd->rwc", src_grad, out_weight, preferred_element_type=jnp.float32)
    block_grad = jnp.where(relu_rows > 0, hidden, 0.0).astype(jnp.bfloat16)
    out_term = jnp.einsum("rwc,rwd->cd", relu_rows, src_grad, preferred_element_type=jnp.float32)
    return (block_grad, out_term)


def conv_back(grad_pad, inputs, kernel):
    row_total = inputs.shape[0]
    width_total = inputs.shape[1]
    padded = jnp.pad(grad_pad, ((0, 0), (1, 1), (0, 0)))
    act_sum = jnp.zeros(inputs.shape, jnp.float32)
    tap_grads = []
    for row_tap in range(3):
        for col_tap in range(3):
            window = padded[
                2 - row_tap : 2 - row_tap + row_total, 2 - col_tap : 2 - col_tap + width_total
            ]
            act_sum = act_sum + jnp.einsum(
                "rwo,io->rwi", window, kernel[row_tap, col_tap], preferred_element_type=jnp.float32
            )
            tap_grads.append(
                jnp.einsum("rwi,rwo->io", inputs, window, preferred_element_type=jnp.float32)
            )
    channels = inputs.shape[2]
    return (act_sum, jnp.stack(tap_grads).reshape(3, 3, channels, channels))


def body(upstream, centers, post_relu, conv_input, target_feats, out_weight, conv_weight):
    src_rows, src_width, lookups = upstream.shape
    tgt_rows, tgt_width, feat_width = target_feats.shape
    channels = post_relu.shape[2]
    src_devices = lax.axis_size("src")
    tgt_devices = lax.axis_size("tgt")
    row_first = lax.axis_index("tgt") * tgt_rows
    inv_root = 1.0 / math.sqrt(feat_width)
    source_total = src_rows * src_width
    flat_grads = upstream.reshape(source_total, lookups)
    flat_rows = centers[0].reshape(source_total)
    flat_cols = centers[1].reshape(source_total)
    block_size = math.gcd(256, source_total)

    def build_block(block_no):
        first_row = block_no * block_size
        return corr_block(
            lax.dynamic_slice_in_dim(flat_rows, first_row, block_size),
            lax.dynamic_slice_in_dim(flat_cols, first_row, block_size),
            lax.dynamic_slice_in_dim(flat_grads, first_row, block_size, 0),
            row_first,
            tgt_rows,
            tgt_width,
        )

    corr_grad = lax.map(build_block, jnp.arange(source_total // block_size, dtype=jnp.int32))
    corr_grad = corr_grad.reshape(source_total, tgt_rows, tgt_width)
    corr_flat = corr_grad.reshape(source_total, tgt_rows * tgt_width)
    src_feats = jnp.dot(
        post_relu.reshape(source_total, channels), out_weight, preferred_element_type=jnp.float32
    ).astype(jnp.bfloat16)
    flat_targets = target_feats.reshape(tgt_rows * tgt_width, feat_width)
    corr_piece = lax.slice_in_dim(
        corr_grad, 0, tgt_width // src_devices * lax.axis_size("src"), axis=2
    )
    target_share = lax.psum_scatter(
        jnp.einsum("syc,sd->cyd", corr_piece, src_feats, preferred_element_type=jnp.float32)
        * inv_root,
        "src",
        scatter_dimension=0,
        tiled=True,
    )
    tgt_grad = jnp.transpose(target_share, (1, 0, 2)).astype(jnp.bfloat16)
    tile_rows = src_rows // tgt_devices
    corr_piece = lax.dynamic_slice_in_dim(
        corr_flat, jnp.int32(0) * src_width, tile_rows * lax.axis_size("tgt") * src_width, 0
    )
    product = jnp.dot(corr_piece, flat_targets, preferred_element_type=jnp.float32) * inv_root
    src_grad = lax.psum_scatter(
        product.reshape(tile_rows * lax.axis_size("tgt"), src_width, feat_width),
        "tgt",
        scatter_dimension=0,
        tiled=True,
    ).astype(jnp.bfloat16)
    relu_tile = lax.dynamic_slice_in_dim(post_relu, lax.axis_index("tgt") * tile_rows, tile_rows, 0)
    block_grad, out_term = hidden_grads(src_grad, relu_tile, out_weight)
    grad_pad = padded_2(block_grad, ((("src", "tgt"), 0),), 1)
    act_sum, conv_term = conv_back(grad_pad, conv_input, conv_weight)
    out_total, conv_total = lax.psum((out_term, conv_term), ("src", "tgt"))
    act_grad = act_sum.astype(jnp.bfloat16)
    row_count = float(src_rows * src_devices)
    return (tgt_grad, act_grad, out_total / row_count, conv_total / row_count)


def solution(mesh):
    placed = (
        P("src", None, None),
        P(None, "src", None),
        P("src", None, None),
        P(("src", "tgt"), None, None),
        P("tgt", None, None),
        P(),
        P(),
    )
    return jax.shard_map(
        body,
        mesh=mesh,
        in_specs=placed,
        out_specs=(P("tgt", "src", None), P(("src", "tgt"), None, None), P(), P()),
        check_vma=False,
    )
```

profile of v0, /device:TPU:0, one launch (start us, length us, event | category | flops | bytes accessed | tf_op | source)
XLA Modules:
  0.0 281.5 jit_solution(11257590945642890036)
XLA Ops:
  8.9 1.1 pad.23
  10.1 84.5 %while.13 = (s32[]{:T(128)}, bf16[4,256,8,256]{3,2,1,0:T(8,128)(2,1)}, s32[]{:T(128)}, s32[4]{0:T(128)S(1)}, s32[1024]{0:T(1024)S(1)}, /*index=5*/bf16[1024,324]...) while((s32[]{:T(128)}, ...), condition=%wide.region_1.2_spmd, body=%wide.region_0.1_spmd.sunk | while | flops 104745304 | bytes 30385264 | solution.py:112
  12.7 1.0 copy.82
  13.7 2.1 fusion.168
  15.9 1.0 copy.83
  16.9 2.1 fusion.169
  19.2 1.0 copy.85
  20.2 2.0 fusion.171
  22.4 1.0 copy.84
  25.6 5.7 %fusion.172 = bf16[4,256,8,256]{3,2,1,0:T(8,128)(2,1)} fusion(bf16[4,256,8,256]{3,2,1,0:T(8,128)(2,1)} %get-tuple-element.286, s32[]{:T(128)} %get-tuple-element.285, bf16[256,36,8]{1,2,0:T(8,128)(2,1)S(1)} %copy.81, bf16[256,9,256]{2,1,0:T(8,128)(2,1)S(1)} %copy-done.7, bf16[256,9,256]{2,1,0:T(8,128)(2,1)S(1)} %copy-done.8, ...), kind=kOutput, calls=%fused_computation.34.clone.1 | convolution fusion | flops 56623104 | bytes 6832640 | tf_op jit(solution)/shard_map/while/body/eval_jaxpr/say,sax->syx/dot_general | solution.py:56
  33.8 1.0 copy.82
  34.9 2.1 fusion.168
  37.1 1.0 copy.83
  38.1 2.1 fusion.169
  40.3 1.0 copy.85
  41.3 2.0 fusion.171
  43.5 1.0 copy.84
  46.7 5.7 %fusion.172 = bf16[4,256,8,256]{3,2,1,0:T(8,128)(2,1)} fusion(bf16[4,256,8,256]{3,2,1,0:T(8,128)(2,1)} %get-tuple-element.286, s32[]{:T(128)} %get-tuple-element.285, bf16[256,36,8]{1,2,0:T(8,128)(2,1)S(1)} %copy.81, bf16[256,9,256]{2,1,0:T(8,128)(2,1)S(1)} %copy-done.7, bf16[256,9,256]{2,1,0:T(8,128)(2,1)S(1)} %copy-done.8, ...), kind=kOutput, calls=%fused_computation.34.clone.1 | convolution fusion | flops 56623104 | bytes 6832640 | tf_op jit(solution)/shard_map/while/body/eval_jaxpr/say,sax->syx/dot_general | solution.py:56
  55.0 1.0 copy.82
  56.0 2.1 fusion.168
  58.2 1.0 copy.83
  59.2 2.1 fusion.169
  61.4 1.0 copy.85
  62.4 2.0 fusion.171
  64.6 1.0 copy.84
  67.9 5.7 %fusion.172 = bf16[4,256,8,256]{3,2,1,0:T(8,128)(2,1)} fusion(bf16[4,256,8,256]{3,2,1,0:T(8,128)(2,1)} %get-tuple-element.286, s32[]{:T(128)} %get-tuple-element.285, bf16[256,36,8]{1,2,0:T(8,128)(2,1)S(1)} %copy.81, bf16[256,9,256]{2,1,0:T(8,128)(2,1)S(1)} %copy-done.7, bf16[256,9,256]{2,1,0:T(8,128)(2,1)S(1)} %copy-done.8, ...), kind=kOutput, calls=%fused_computation.34.clone.1 | convolution fusion | flops 56623104 | bytes 6832640 | tf_op jit(solution)/shard_map/while/body/eval_jaxpr/say,sax->syx/dot_general | solution.py:56
  76.1 1.0 copy.82
  77.1 2.1 fusion.168
  79.3 1.0 copy.83
  80.3 2.1 fusion.169
  82.6 1.0 copy.85
  83.6 2.0 fusion.171
  85.7 1.0 copy.84
  89.0 5.7 %fusion.172 = bf16[4,256,8,256]{3,2,1,0:T(8,128)(2,1)} fusion(bf16[4,256,8,256]{3,2,1,0:T(8,128)(2,1)} %get-tuple-element.286, s32[]{:T(128)} %get-tuple-element.285, bf16[256,36,8]{1,2,0:T(8,128)(2,1)S(1)} %copy.81, bf16[256,9,256]{2,1,0:T(8,128)(2,1)S(1)} %copy-done.7, bf16[256,9,256]{2,1,0:T(8,128)(2,1)S(1)} %copy-done.8, ...), kind=kOutput, calls=%fused_computation.34.clone.1 | convolution fusion | flops 56623104 | bytes 6832640 | tf_op jit(solution)/shard_map/while/body/eval_jaxpr/say,sax->syx/dot_general | solution.py:56
  94.7 3.7 %copy.71 = bf16[128,8,8,256]{3,1,2,0:T(8,128)(2,1)S(1)} copy(bf16[128,8,8,256]{3,2,1,0:T(8,128)(2,1)} %bitcast.96) | data formatting | bytes 8388608
  98.4 2.3 convolution_multiply_fusion
  100.7 23.1 %reduce-scatter.5.cloned.1.call-done = f32[4,128,256]{2,1,0:T(8,128)} async-done(((f32[8,128,256]{2,1,0:T(8,128)}), f32[4,128,256]{2,1,0:T(8,128)}) %reduce-scatter.5.cloned.1.call-update) | async-done | bytes 524304 | tf_op jit(solution)/shard_map/reduce_scatter | solution.py:135
  123.9 1.3 fusion.56
  125.2 2.2 collective-permute-start
  127.4 1.5 collective-permute-start.1
  128.9 1.9 convolution_bitcast_fusion
  130.8 2.7 collective-permute-done.1
  135.7 1.1 copy.56
  136.8 4.3 %multiply_bitcast_fusion = f32[256,8,256]{0,2,1:T(8,128)S(1)} fusion(bf16[1024,8,256]{2,1,0:T(8,128)(2,1)} %bitcast.6, bf16[1024,128]{1,0:T(8,128)(2,1)} %bitcast.201, bf16[128,256]{1,0:T(8,128)(2,1)} %param.14), kind=kOutput, calls=%fused_computation.111 | convolution fusion | flops 1141637120 | bytes 6619136 | tf_op jit(solution)/shard_map/syc,sd->cyd/dot_general | solution.py:123
  141.2 2.0 copy.45
  148.7 120.4 %all-reduce.4.cloned.1.call-done = (f32[128,256]{1,0:T(8,128)}, f32[3,3,128,128]{3,2,1,0:T(8,128)}) async-done(((f32[128,256]{1,0:T(8,128)}, f32[3,3,128,128]{3,2,1,0:T(8,128)}), (f32[128,256]{1,0:T(8,128)}, f32[3,3,128,128]{3,2,1,0:T(8,128)})) %all-reduce.4.cloned.1.call-update) | async-done | bytes 720912 | tf_op jit(solution)/shard_map/psum | solution.py:145
  269.1 1.6 broadcast_multiply_fusion.1
  270.6 1.9 broadcast_multiply_fusion
  (192 shorter events, 27.9 us)
Async XLA Ops:
  8.0 90.3 %copy-start = (bf16[8,256,256]{2,1,0:T(8,128)(2,1)S(1)}, bf16[8,256,256]{2,1,0:T(8,128)(2,1)}, u32[]{:S(2)}) copy-start(bf16[8,256,256]{2,1,0:T(8,128)(2,1)} %param.13) | copy-start | bytes 3145732
  8.0 115.8 %reduce-scatter.5.cloned.1.call-start = ((), (), s32[]{:S(2)}) async-start(), calls=%async_computation.3 | async-start | bytes 1572864 | tf_op jit(solution)/shard_map/reduce_scatter | solution.py:135
  10.2 2.5 copy-start.1
  23.4 1.6 copy-start.7
  23.4 2.2 copy-start.8
  25.6 5.7 %copy-start.2 = (bf16[1024,324]{0,1:T(8,128)(2,1)S(1)}, bf16[1024,324]{0,1:T(8,128)(2,1)}, u32[]{:S(2)}) copy-start(bf16[1024,324]{0,1:T(8,128)(2,1)} %copy-done.1) | copy-start | bytes 1990660 | tf_op jit(solution)/shard_map/while
  31.3 2.5 copy-start.1
  44.5 1.6 copy-start.7
  44.5 2.2 copy-start.8
  46.7 5.7 %copy-start.2 = (bf16[1024,324]{0,1:T(8,128)(2,1)S(1)}, bf16[1024,324]{0,1:T(8,128)(2,1)}, u32[]{:S(2)}) copy-start(bf16[1024,324]{0,1:T(8,128)(2,1)} %copy-done.1) | copy-start | bytes 1990660 | tf_op jit(solution)/shard_map/while
  52.4 2.5 copy-start.1
  65.6 1.6 copy-start.7
  65.6 2.2 copy-start.8
  67.9 5.7 %copy-start.2 = (bf16[1024,324]{0,1:T(8,128)(2,1)S(1)}, bf16[1024,324]{0,1:T(8,128)(2,1)}, u32[]{:S(2)}) copy-start(bf16[1024,324]{0,1:T(8,128)(2,1)} %copy-done.1) | copy-start | bytes 1990660 | tf_op jit(solution)/shard_map/while
  73.6 2.5 copy-start.1
  86.8 1.6 copy-start.7
  86.8 2.2 copy-start.8
  89.0 5.7 %copy-start.2 = (bf16[1024,324]{0,1:T(8,128)(2,1)S(1)}, bf16[1024,324]{0,1:T(8,128)(2,1)}, u32[]{:S(2)}) copy-start(bf16[1024,324]{0,1:T(8,128)(2,1)} %copy-done.1) | copy-start | bytes 1990660 | tf_op jit(solution)/shard_map/while
  98.4 25.5 %copy-start.5 = (bf16[8,128,128]{2,1,0:T(8,128)(2,1)S(1)}, bf16[8,128,128]{2,1,0:T(8,128)(2,1)}, u32[]{:S(2)}) copy-start(bf16[8,128,128]{2,1,0:T(8,128)(2,1)} %param.11) | copy-start | bytes 786436
  98.4 25.5 %copy-start.6 = (bf16[128,256]{1,0:T(8,128)(2,1)S(1)}, bf16[128,256]{1,0:T(8,128)(2,1)}, u32[]{:S(2)}) copy-start(bf16[128,256]{1,0:T(8,128)(2,1)} %param.14) | copy-start | bytes 196612
  98.4 35.2 %copy-start.3 = (bf16[4,128,128]{2,1,0:T(8,128)(2,1)S(1)}, bf16[4,128,128]{2,1,0:T(8,128)(2,1)}, u32[]{:S(2)}) copy-start(bf16[4,128,128]{2,1,0:T(8,128)(2,1)} %param.12) | copy-start | bytes 393220
  100.7 168.4 %all-reduce.4.cloned.1.call-start = ((), (), s32[]{:S(2)}) async-start(), calls=%async_computation.4 | async-start | bytes 1441792 | tf_op jit(solution)/shard_map/psum | solution.py:145
  125.2 5.6 %collective-permute-start = (bf16[1,128,128]{2,1,0:T(8,128)(2,1)S(1)}, bf16[1,128,128]{2,1,0:T(8,128)(2,1)S(1)}, u32[]{:S(2)}, u32[]{:S(2)}) collective-permute-start(bf16[1,128,128]{2,1,0:T(8,128)(2,1)S(1)} %get-tuple-element.192), channel_id=1, source_target_pairs={{0,1},{1,2},{2,3},{3,4},{4,5},{5,6},{6,7},{7,8},{8,9},{9,10},{10,1... | collective-permute-start | bytes 98312 | tf_op jit(solution)/shard_map/ppermute | solution.py:16
  127.4 6.1 %collective-permute-start.1 = (bf16[1,128,128]{2,1,0:T(8,128)(2,1)S(1)}, bf16[1,128,128]{2,1,0:T(8,128)(2,1)S(1)}, u32[]{:S(2)}, u32[]{:S(2)}) collective-permute-start(bf16[1,128,128]{2,1,0:T(8,128)(2,1)S(1)} %get-tuple-element.193), channel_id=1, source_target_pairs={{1,0},{2,1},{3,2},{4,3},{5,4},{6,5},{7,6},{8,7},{9,8},{10,9},{11,1... | collective-permute-start | bytes 98312 | tf_op jit(solution)/shard_map/ppermute | solution.py:17
  136.8 135.8 %reduce-scatter.3.cloned.1.call-start = ((), (), s32[]{:S(2)}) async-start(), calls=%async_computation.2 | async-start | bytes 2228224 | tf_op jit(solution)/shard_map/reduce_scatter | solution.py:122
  143.1 3.9 %copy-start.4 = (bf16[3,3,128,128]{3,2,1,0:T(8,128)(2,1)S(1)}, bf16[3,3,128,128]{3,2,1,0:T(8,128)(2,1)}, u32[]{:S(2)}) copy-start(bf16[3,3,128,128]{3,2,1,0:T(8,128)(2,1)} %param.15) | copy-start | bytes 884740
Sparse Core Ops, SparseCore 0:
  100.8 23.0 reduce-scatter.4
  136.9 132.1 all-reduce.3
Sparse Core Ops, SparseCore 1:
  143.3 63.5 reduce-scatter.2
where the time goes:
time: 282 us
  waiting for transfers between devices  146 us (52%)
  matrix products  67.6 us (24%)
  local copies, waits for them, and re-layouts  36.6 us (13%)
  between operations  15.8 us (6%)
  other arithmetic  8.1 us (3%)
  starting transfers between devices  3.81 us (1%)
  loops' own time  3.39 us (1%)
    psum x1, waiting for transfers between devices, body(): out_total, conv_total = lax.psum((out_term, conv_term), ('src', 'tgt'))  120 us
    dot_general x16, matrix products, corr_block(): col_parts.append(jnp.einsum('sab,sbx->sax', level_grads, col_hot))  27.6 us
    reduce_scatter x1, waiting for transfers between devices, body(): lax.psum_scatter(product.reshape(tile_rows * lax.axis_size('tgt'), src_wi...  23.1 us
    dot_general x4, matrix products, corr_block(): return jnp.einsum('say,sax->syx', row_table, col_table).astype(jnp.bfloat16)  22.8 us
    reshape x32, local copies, waits for them, and re-layouts, corr_block(): level_grads = grad_rows[:, 81 * level_no:81 * (level_no + 1)].astype(jnp....  16.4 us
    while x32, local copies, waits for them, and re-layouts  6.05 us
  transfers between devices with their start and end apart: 5, of which 3 were waited for; matrix products, arithmetic and copies ran while one was open for 6% of the time, Pallas kernels for 0%

commit v1 on v0

v1 whole, which is shorter than its diff:
```python
import math

import jax
import jax.numpy as jnp
from jax import lax
from jax.experimental import pallas as pl
from jax.experimental.pallas import tpu as pltpu
from jax.sharding import PartitionSpec as P

OFFSET = (0, 81, 34, 115)
EMPTY = (100, 178, 120, 208)
FAR = 4096


def dot(a, b, dims=((1,), (0,))):
    return lax.dot_general(a, b, (dims, ((), ())), preferred_element_type=jnp.float32)


def spread_matrix(half, width, transposed):
    shape = (384, width) if transposed else (width, 384)
    cell = lax.broadcasted_iota(jnp.int32, shape, 0 if transposed else 1)
    col = lax.broadcasted_iota(jnp.int32, shape, 1 if transposed else 0)
    one = jnp.where(cell == (col >> 1), 0.25, 0.0)
    two = jnp.where(cell == 128 + 64 * half + (col >> 2), 0.0625, 0.0)
    three = jnp.where(cell == 256 + (col >> 3), 0.015625, 0.0)
    return (one + two + three).astype(jnp.bfloat16)


def build_table(row_first, up_ref, cen_ref, rows_ref, cols_ref, tail_ref, table_ref):
    total = up_ref.shape[0]
    for r in range(total // 128):
        for part, ref in ((0, rows_ref), (1, cols_ref)):
            line = jnp.broadcast_to(cen_ref[part, r : r + 1, :], (128, 128))
            ref[r * 128 : (r + 1) * 128, :] = jnp.transpose(line)
    tail_ref[:, 0:68] = up_ref[:, 256:324].astype(jnp.float32)
    lane = lax.broadcasted_iota(jnp.int32, (16, 128), 1)

    @pl.loop(0, total // 16)
    def _(group):
        here = pl.ds(pl.multiple_of(group * 16, 16), 16)
        first = up_ref[here, 0:128].astype(jnp.float32)
        second = up_ref[here, 128:256].astype(jnp.float32)
        third = tail_ref[here, :]
        source = (
            jnp.where(lane < 81, first, 0.0),
            jnp.where(lane >= 81, first, jnp.where(lane < 34, second, 0.0)),
            jnp.where((lane >= 34) & (lane < 115), second, 0.0),
            jnp.where(lane >= 115, second, jnp.where(lane < 68, third, 0.0)),
        )
        center_row = rows_ref[here, :]
        center_col = cols_ref[here, :]

        def row_term(level, cell):
            a = cell + ((row_first >> level) + 4) - (center_row >> level)
            return jnp.where((a >= 0) & (a < 9), 9 * a + OFFSET[level], FAR)

        def col_term(level, cell):
            b = cell + 4 - (center_col >> level)
            return jnp.where((b >= 0) & (b < 9), b, FAR)

        def put(level, tile, index):
            index = jnp.minimum(index, EMPTY[level]) & 127
            value = jnp.take_along_axis(source[level], index, axis=1, mode="promise_in_bounds")
            table_ref[here, tile * 128 : (tile + 1) * 128] = value.astype(jnp.bfloat16)

        halves = [col_term(0, lane + 128 * h) for h in range(2)]
        for y in range(8):
            a = row_term(0, y)
            for h in range(2):
                put(0, 2 * y + h, a + halves[h])
        b = col_term(1, lane)
        for j in range(4):
            put(1, 16 + j, row_term(1, j) + b)
        put(2, 20, row_term(2, lane >> 6) + col_term(2, lane & 63))
        put(3, 21, jnp.where(lane < 32, row_term(3, 0) + col_term(3, lane), FAR))


def corr_kernel(
    up_ref, cen_ref, relu_ref, tf_ref, ow_ref,
    src_ref, tgt_ref,
    rows_ref, cols_ref, tail_ref, table_ref, pooled_ref, sums_ref, feats_ref,
):
    total = up_ref.shape[0]
    width = tf_ref.shape[1]
    feat = tf_ref.shape[2]
    dense = tf_ref.shape[0] * width
    scale = 1.0 / math.sqrt(feat)
    row_first = lax.axis_index("tgt") * tf_ref.shape[0]
    build_table(row_first, up_ref, cen_ref, rows_ref, cols_ref, tail_ref, table_ref)

    mats = [spread_matrix(half, width, True) for half in range(2)]
    coarse = jnp.zeros((256, feat), jnp.float32)
    for j in range(4):
        fine = jnp.zeros((128, feat), jnp.float32)
        for y in (2 * j, 2 * j + 1):
            part = dot(mats[y // 4], tf_ref[y])
            fine = fine + part[:128]
            coarse = coarse + part[128:]
        pooled_ref[j * 128 : (j + 1) * 128, :] = fine.astype(jnp.bfloat16)
    pooled_ref[512:768, :] = coarse.astype(jnp.bfloat16)

    feats_ref[...] = dot(ow_ref[...], relu_ref[...], ((0,), (1,))).astype(jnp.bfloat16)

    @pl.loop(0, total // 256)
    def _(block):
        here = pl.ds(pl.multiple_of(block * 256, 256), 256)
        value = dot(table_ref[here, :dense], tf_ref[...].reshape(dense, feat))
        value = value + dot(table_ref[here, dense:], pooled_ref[...])
        src_ref[here, :] = (value * scale).astype(src_ref.dtype)

    @pl.loop(0, table_ref.shape[1] // 256)
    def _(tile):
        here = pl.ds(pl.multiple_of(tile * 256, 256), 256)
        sums_ref[:, here] = dot(feats_ref[...], table_ref[:, here]).astype(jnp.bfloat16)

    eye = (
        lax.broadcasted_iota(jnp.int32, (width, width), 0)
        == lax.broadcasted_iota(jnp.int32, (width, width), 1)
    )
    eye = jnp.where(eye, 1.0, 0.0).astype(jnp.bfloat16)
    for y in range(8):
        mat = spread_matrix(y // 4, width, False)
        j = y // 2
        value = dot(eye, sums_ref[:, y * 256 : (y + 1) * 256], ((1,), (1,)))
        value = value + dot(
            mat[:, :128], sums_ref[:, dense + j * 128 : dense + (j + 1) * 128], ((1,), (1,))
        )
        value = value + dot(mat[:, 128:], sums_ref[:, dense + 512 :], ((1,), (1,)))
        tgt_ref[y] = (value * scale).astype(tgt_ref.dtype)


def corr_grads(upstream, centers, post_relu, target_feats, out_weight):
    total = upstream.shape[0] * upstream.shape[1]
    rows, width, feat = target_feats.shape
    assert rows == 8 and width == 256
    cells = rows * width + 768
    vmem = pl.BlockSpec(memory_space=pltpu.VMEM)
    return pl.pallas_call(
        corr_kernel,
        out_shape=(
            jax.ShapeDtypeStruct((total, feat), jnp.float32),
            jax.ShapeDtypeStruct((rows, width, feat), jnp.float32),
        ),
        in_specs=[vmem] * 5,
        out_specs=(vmem, vmem),
        scratch_shapes=[
            pltpu.VMEM((total, 128), jnp.int32),
            pltpu.VMEM((total, 128), jnp.int32),
            pltpu.VMEM((total, 128), jnp.float32),
            pltpu.VMEM((total, cells), jnp.bfloat16),
            pltpu.VMEM((768, feat), jnp.bfloat16),
            pltpu.VMEM((feat, cells), jnp.bfloat16),
            pltpu.VMEM((feat, total), jnp.bfloat16),
        ],
        compiler_params=pltpu.CompilerParams(vmem_limit_bytes=48 * 2**20),
        cost_estimate=pl.CostEstimate(
            flops=4 * total * cells * feat, bytes_accessed=6 * 2**20, transcendentals=0
        ),
    )(
        upstream.reshape(total, -1),
        centers,
        post_relu.reshape(total, -1),
        target_feats,
        out_weight,
    )


def padded_2(array, sides, width):
    for axis, dim in sides:
        devices, length = (lax.axis_size(axis), array.shape[dim])
        up = [(i, (i + 1) % devices) for i in range(devices - 1)]
        down = [(j, i) for i, j in up]
        last = lax.slice_in_dim(array, length - width, length, axis=dim)
        first = lax.slice_in_dim(array, 0, width, axis=dim)
        before = lax.ppermute(last, axis, up)
        after = lax.ppermute(first, axis, down)
        array = jnp.concatenate([before, array, after], axis=dim)
    return array


def hidden_grads(src_grad, relu_rows, out_weight):
    hidden = jnp.einsum("rwd,cd->rwc", src_grad, out_weight, preferred_element_type=jnp.float32)
    block_grad = jnp.where(relu_rows > 0, hidden, 0.0).astype(jnp.bfloat16)
    out_term = jnp.einsum("rwc,rwd->cd", relu_rows, src_grad, preferred_element_type=jnp.float32)
    return (block_grad, out_term)


def conv_back(grad_pad, inputs, kernel):
    row_total = inputs.shape[0]
    width_total = inputs.shape[1]
    padded = jnp.pad(grad_pad, ((0, 0), (1, 1), (0, 0)))
    act_sum = jnp.zeros(inputs.shape, jnp.float32)
    tap_grads = []
    for row_tap in range(3):
        for col_tap in range(3):
            window = padded[
                2 - row_tap : 2 - row_tap + row_total, 2 - col_tap : 2 - col_tap + width_total
            ]
            act_sum = act_sum + jnp.einsum(
                "rwo,io->rwi", window, kernel[row_tap, col_tap], preferred_element_type=jnp.float32
            )
            tap_grads.append(
                jnp.einsum("rwi,rwo->io", inputs, window, preferred_element_type=jnp.float32)
            )
    channels = inputs.shape[2]
    return (act_sum, jnp.stack(tap_grads).reshape(3, 3, channels, channels))


def body(upstream, centers, post_relu, conv_input, target_feats, out_weight, conv_weight):
    src_rows, src_width, lookups = upstream.shape
    feat_width = target_feats.shape[2]
    src_devices = lax.axis_size("src")
    tgt_devices = lax.axis_size("tgt")
    product, target = corr_grads(upstream, centers, post_relu, target_feats, out_weight)
    target_share = lax.psum_scatter(target, "src", scatter_dimension=1, tiled=True)
    tgt_grad = target_share.astype(jnp.bfloat16)
    tile_rows = src_rows // tgt_devices
    src_grad = lax.psum_scatter(
        product.reshape(src_rows, src_width, feat_width),
        "tgt",
        scatter_dimension=0,
        tiled=True,
    ).astype(jnp.bfloat16)
    relu_tile = lax.dynamic_slice_in_dim(post_relu, lax.axis_index("tgt") * tile_rows, tile_rows, 0)
    block_grad, out_term = hidden_grads(src_grad, relu_tile, out_weight)
    grad_pad = padded_2(block_grad, ((("src", "tgt"), 0),), 1)
    act_sum, conv_term = conv_back(grad_pad, conv_input, conv_weight)
    out_total, conv_total = lax.psum((out_term, conv_term), ("src", "tgt"))
    act_grad = act_sum.astype(jnp.bfloat16)
    row_count = float(src_rows * src_devices)
    return (tgt_grad, act_grad, out_total / row_count, conv_total / row_count)


def solution(mesh):
    placed = (
        P("src", None, None),
        P(None, "src", None),
        P("src", None, None),
        P(("src", "tgt"), None, None),
        P("tgt", None, None),
        P(),
        P(),
    )
    return jax.shard_map(
        body,
        mesh=mesh,
        in_specs=placed,
        out_specs=(P("tgt", "src", None), P(("src", "tgt"), None, None), P(), P()),
        check_vma=False,
    )
```

time: 282 us -> 218 us (0.77)
  matrix products: 67.6 us -> 7.59 us
  local copies, waits for them, and re-layouts: 36.6 us -> 6.36 us
  Pallas kernels: 0 us -> 21.9 us
  waiting for transfers between devices: 146 us -> 155 us
  loops' own time: 3.39 us -> 0 us
  other arithmetic: 8.1 us -> 5.1 us
    dot_general x22 -> x0, matrix products: 56.9 us -> none  [the longest x16 27.6 us: corr_block(): col_parts.append(jnp.einsum('sab,sbx->sax', level_grads, col_hot))]
    pallas_call x0 -> x1, Pallas kernels: none -> 21.9 us  [corr_grads(): pl.pallas_call(corr_kernel, out_shape=(jax.ShapeDtypeStruct((total, feat)...]
    reshape x32 -> x0, local copies, waits for them, and re-layouts: 16.4 us -> none  [corr_block(): level_grads = grad_rows[:, 81 * level_no:81 * (level_no + 1)].astype(jnp....]
    psum x1, waiting for transfers between devices: 120 us -> 132 us  [body(): out_total, conv_total = lax.psum((out_term, conv_term), ('src', 'tgt'))]
    while x32 -> x0, local copies, waits for them, and re-layouts: 6.05 us -> none
    another operation x1 -> x0, loops' own time: 3.39 us -> none  [body(): lax.map(build_block, jnp.arange(source_total // block_size, dtype=jnp.int...]
    dot_general x9, matrix products: 5.42 us -> 2.34 us  [conv_back(): jnp.einsum('rwo,io->rwi', window, kernel[row_tap, col_tap], preferred_ele...]
  transfers between devices with their start and end apart: 5 -> 5, of which waited for: 3 -> 2; matrix products, arithmetic and copies ran while one was open for 6% -> 4% of each run, Pallas kernels for 0% -> 0%
where the time goes in v1:
time: 218 us
  waiting for transfers between devices  155 us (71%)
  Pallas kernels  21.9 us (10%)
  between operations  15.7 us (7%)
  matrix products  7.59 us (3%)
  local copies, waits for them, and re-layouts  6.36 us (3%)
  starting transfers between devices  5.96 us (3%)
  other arithmetic  5.1 us (2%)
    psum x1, waiting for transfers between devices, body(): out_total, conv_total = lax.psum((out_term, conv_term), ('src', 'tgt'))  132 us
    reduce_scatter x1, waiting for transfers between devices, body(): lax.psum_scatter(product.reshape(src_rows, src_width, feat_width), 'tgt',...  23.1 us
    pallas_call x1, Pallas kernels, corr_grads(): pl.pallas_call(corr_kernel, out_shape=(jax.ShapeDtypeStruct((total, feat)...  21.9 us
    unnamed x17, local copies, waits for them, and re-layouts  5.31 us
    ppermute x1, starting transfers between devices, padded_2(): before = lax.ppermute(last, axis, up)  4.55 us
  transfers between devices with their start and end apart: 5, of which 2 were waited for; matrix products, arithmetic and copies ran while one was open for 4% of the time, Pallas kernels for 0%

profile of v1, /device:TPU:0, one launch (start us, length us, event | category | flops | bytes accessed | tf_op | source)
XLA Modules:
  0.0 217.9 jit_solution(12204576000110233146)
XLA Ops:
  8.0 0.0 copy-start
  8.0 0.0 reduce-scatter.5.cloned.1.call-start
  8.1 1.6 copy.11
  9.6 0.0 copy-start.1
  9.7 0.9 copy-done.1
  10.6 0.8 copy-done.3
  11.4 1.2 copy-done.5
  12.7 0.7 copy-done.6
  13.4 21.9 %shard_map.102 = (f32[1024,256]{1,0:T(8,128)}, f32[8,256,256]{2,1,0:T(8,128)}) custom-call(bf16[1024,324]{1,0:T(8,128)(2,1)S(1)} %bitcast.137, s32[2,8,128]{2,1,0:T(8,128)S(1)} %copy-done.6, bf16[1024,128]{1,0:T(8,128)(2,1)S(1)} %bitcast.138, bf16[8,256,256]{2,1,0:T(8,128)(2,1)S(1)} %copy-done.5, bf16[128,256]{1,0:T(8,128)(2,1)S(1)} %copy-done.3), custom_call_target="tpu_custom_call" | custom-call | flops 2952790016 | bytes 6291456 | tf_op jit(solution)/shard_map/pallas_call | solution.py:138
  35.3 0.0 reduce-scatter.5.cloned.1.call-update
  35.3 0.0 all-reduce.4.cloned.1.call-start
  35.3 23.1 %reduce-scatter.5.cloned.1.call-done = f32[4,128,256]{2,1,0:T(8,128)} async-done(((f32[8,128,256]{2,1,0:T(8,128)}), f32[4,128,256]{2,1,0:T(8,128)}) %reduce-scatter.5.cloned.1.call-update) | async-done | bytes 524304 | tf_op jit(solution)/shard_map/reduce_scatter | solution.py:218
  58.4 0.0 copy-done.2
  58.4 0.0 copy-done.4
  58.4 1.3 fusion.1
  59.7 1.3 collective-permute-start.1
  61.0 4.5 %collective-permute-start = (bf16[1,128,128]{2,1,0:T(8,128)(2,1)S(1)}, bf16[1,128,128]{2,1,0:T(8,128)(2,1)S(1)}, u32[]{:S(2)}, u32[]{:S(2)}) collective-permute-start(bf16[1,128,128]{2,1,0:T(8,128)(2,1)S(1)} %get-tuple-element.10), channel_id=1, source_target_pairs={{0,1},{1,2},{2,3},{3,4},{4,5},{5,6},{6,7},{7,8},{8,9},{9,10},{10,1... | collective-permute-start | bytes 98312 | tf_op jit(solution)/shard_map/ppermute | solution.py:175
  65.6 1.9 convolution_bitcast_fusion
  67.5 0.0 collective-permute-done.1
  67.5 0.0 collective-permute-done
  67.5 0.1 fusion.17
  67.6 0.2 fusion.11
  67.8 0.2 fusion.4
  68.1 0.2 fusion.10
  68.3 0.2 fusion.9
  68.6 0.2 fusion.8
  68.8 0.2 fusion.7
  69.0 0.2 fusion.6
  69.3 0.2 fusion.3
  69.5 0.0 copy-start.7
  69.5 0.2 fusion.5
  69.7 1.1 copy.22
  70.8 0.0 all-reduce.4.cloned.1.call-update
  70.8 0.0 reduce-scatter.3.cloned.1.call-start
  70.9 0.5 reduce-scatter.3.cloned.1.call-update
  71.4 0.2 fusion.34
  71.6 0.2 fusion.21
  71.8 0.2 convolution_add_fusion.6
  72.0 0.2 convolution_add_fusion.5
  72.2 0.2 convolution_add_fusion.4
  72.4 0.2 convolution_add_fusion.3
  72.6 0.2 convolution_add_fusion.2
  72.8 0.2 convolution_add_fusion.1
  72.9 0.8 fusion.2
  73.8 131.6 %all-reduce.4.cloned.1.call-done = (f32[128,256]{1,0:T(8,128)}, f32[3,3,128,128]{3,2,1,0:T(8,128)}) async-done(((f32[128,256]{1,0:T(8,128)}, f32[3,3,128,128]{3,2,1,0:T(8,128)}), (f32[128,256]{1,0:T(8,128)}, f32[3,3,128,128]{3,2,1,0:T(8,128)})) %all-reduce.4.cloned.1.call-update) | async-done | bytes 720912 | tf_op jit(solution)/shard_map/psum | solution.py:228
  205.4 1.6 broadcast_multiply_fusion.1
  207.0 1.9 broadcast_multiply_fusion
  208.9 1.5 convert_element_type.14
  (9 shorter events, 0.0 us)
Async XLA Ops:
  8.0 59.6 %copy-start = (bf16[4,128,128]{2,1,0:T(8,128)(2,1)S(1)}, bf16[4,128,128]{2,1,0:T(8,128)(2,1)}, u32[]{:S(2)}) copy-start(bf16[4,128,128]{2,1,0:T(8,128)(2,1)} %param.10) | copy-start | bytes 393220
  8.0 50.4 %reduce-scatter.5.cloned.1.call-start = ((), (), s32[]{:S(2)}) async-start(), calls=%async_computation.3 | async-start | bytes 1572864 | tf_op jit(solution)/shard_map/reduce_scatter | solution.py:218
  9.6 1.0 copy-start.1
  10.6 0.8 copy-start.3
  11.4 1.2 copy-start.5
  12.7 0.7 copy-start.6
  13.4 45.1 %copy-start.2 = (bf16[8,128,128]{2,1,0:T(8,128)(2,1)S(1)}, bf16[8,128,128]{2,1,0:T(8,128)(2,1)}, u32[]{:S(2)}) copy-start(bf16[8,128,128]{2,1,0:T(8,128)(2,1)} %param.9) | copy-start | bytes 786436
  13.4 45.1 %copy-start.4 = (bf16[128,256]{1,0:T(8,128)(2,1)S(1)}, bf16[128,256]{1,0:T(8,128)(2,1)}, u32[]{:S(2)}) copy-start(bf16[128,256]{1,0:T(8,128)(2,1)} %ow_ref.1) | copy-start | bytes 196612
  35.3 170.2 %all-reduce.4.cloned.1.call-start = ((), (), s32[]{:S(2)}) async-start(), calls=%async_computation.4 | async-start | bytes 1441792 | tf_op jit(solution)/shard_map/psum | solution.py:228
  59.7 7.8 %collective-permute-start.1 = (bf16[1,128,128]{2,1,0:T(8,128)(2,1)S(1)}, bf16[1,128,128]{2,1,0:T(8,128)(2,1)S(1)}, u32[]{:S(2)}, u32[]{:S(2)}) collective-permute-start(bf16[1,128,128]{2,1,0:T(8,128)(2,1)S(1)} %get-tuple-element.11), channel_id=1, source_target_pairs={{1,0},{2,1},{3,2},{4,3},{5,4},{6,5},{7,6},{8,7},{9,8},{10,9},{11,1... | collective-permute-start | bytes 98312 | tf_op jit(solution)/shard_map/ppermute | solution.py:176
  61.0 6.5 %collective-permute-start = (bf16[1,128,128]{2,1,0:T(8,128)(2,1)S(1)}, bf16[1,128,128]{2,1,0:T(8,128)(2,1)S(1)}, u32[]{:S(2)}, u32[]{:S(2)}) collective-permute-start(bf16[1,128,128]{2,1,0:T(8,128)(2,1)S(1)} %get-tuple-element.10), channel_id=1, source_target_pairs={{0,1},{1,2},{2,3},{3,4},{4,5},{5,6},{6,7},{7,8},{8,9},{9,10},{10,1... | collective-permute-start | bytes 98312 | tf_op jit(solution)/shard_map/ppermute | solution.py:175
  69.5 1.9 copy-start.7
  70.8 138.1 %reduce-scatter.3.cloned.1.call-start = ((), (), s32[]{:S(2)}) async-start(), calls=%async_computation.2 | async-start | bytes 2228224 | tf_op jit(solution)/shard_map/reduce_scatter | solution.py:215
Sparse Core Ops, SparseCore 0:
  35.4 22.9 reduce-scatter.4
  70.9 134.4 all-reduce.3
Sparse Core Ops, SparseCore 1:
  75.0 63.4 reduce-scatter.2

commit v2 on v1

--- a/solution.py
+++ b/solution.py
@@ -10,6 +10,8 @@
 OFFSET = (0, 81, 34, 115)
 EMPTY = (100, 178, 120, 208)
 FAR = 4096
+PIECES = 2
+MESH = pl.DeviceIdType.MESH
 
 
 def dot(a, b, dims=((1,), (0,))):
@@ -126,10 +128,15 @@
             mat[:, :128], sums_ref[:, dense + j * 128 : dense + (j + 1) * 128], ((1,), (1,))
         )
         value = value + dot(mat[:, 128:], sums_ref[:, dense + 512 :], ((1,), (1,)))
-        tgt_ref[y] = (value * scale).astype(tgt_ref.dtype)
-
-
-def corr_grads(upstream, centers, post_relu, target_feats, out_weight):
+        value = (value * scale).astype(tgt_ref.dtype)
+        pieces, _, _, groups, lines, share, _ = tgt_ref.shape
+        for k in range(4 * groups):
+            tgt_ref[y // lines, k % 2, k // 2 % 2, k // 4, y % lines] = value[
+                k * share : (k + 1) * share
+            ]
+
+
+def corr_grads(upstream, centers, post_relu, target_feats, out_weight, devices):
     total = upstream.shape[0] * upstream.shape[1]
     rows, width, feat = target_feats.shape
     assert rows == 8 and width == 256
@@ -138,8 +145,10 @@
     return pl.pallas_call(
         corr_kernel,
         out_shape=(
-            jax.ShapeDtypeStruct((total, feat), jnp.float32),
-            jax.ShapeDtypeStruct((rows, width, feat), jnp.float32),
+            jax.ShapeDtypeStruct((total, feat), jnp.bfloat16),
+            jax.ShapeDtypeStruct(
+                (PIECES, 2, 2, devices // 4, rows // PIECES, width // devices, feat), jnp.bfloat16
+            ),
         ),
         in_specs=[vmem] * 5,
         out_specs=(vmem, vmem),
@@ -165,6 +174,229 @@
     )
 
 
+def shift(value, step, size):
+    return lax.rem(value + step, size)
+
+
+def exchange_kernel(
+    devices, teams, prod_ref, part_ref, src_ref, tgt_ref,
+    got_core, got_pair, got_far, got_src, sum_core, sum_pair,
+    core_send, core_recv, pair_send, pair_recv, far_send, far_recv, src_send, src_recv,
+):
+    s = lax.axis_index("src")
+    t = lax.axis_index("tgt")
+    groups = devices // 4
+    core, pair, far = lax.rem(s, 2), lax.rem(s // 2, 2), s // 4
+    core_mate = (s + 1 - 2 * core, t)
+    pair_mate = (s + 2 - 4 * pair, t)
+
+    def far_mate(d):
+        return (shift(far, d, groups) * 4 + pair * 2 + core, t)
+
+    mates = [core_mate, pair_mate]
+    mates += [far_mate(d) for d in range(1, groups)]
+    mates += [(s, shift(t, d, teams)) for d in range(1, teams)]
+    barrier = pltpu.get_barrier_semaphore()
+    for mate in mates:
+        pl.semaphore_signal(barrier, inc=1, device_id=mate, device_id_type=MESH)
+    pl.semaphore_wait(barrier, len(mates))
+
+    def send(src, dst, send_sem, recv_sem, mate):
+        copy = pltpu.make_async_remote_copy(
+            src_ref=src, dst_ref=dst, send_sem=send_sem, recv_sem=recv_sem,
+            device_id=mate, device_id_type=MESH,
+        )
+        copy.start()
+        return copy
+
+    core_copies = [
+        send(part_ref.at[q, 1 - core], got_core.at[q], core_send.at[q], core_recv.at[q], core_mate)
+        for q in range(PIECES)
+    ]
+    src_copies = [
+        send(
+            prod_ref.at[shift(t, d, teams)], got_src.at[d - 1],
+            src_send.at[d - 1], src_recv.at[d - 1], (s, shift(t, d, teams)),
+        )
+        for d in range(1, teams)
+    ]
+    pair_copies = []
+    for q in range(PIECES):
+        core_copies[q].wait()
+        for half in range(2):
+            value = part_ref[q, core, half].astype(jnp.float32)
+            value = value + got_core[q, half].astype(jnp.float32)
+            sum_core[q, half] = value.astype(jnp.bfloat16)
+        pair_copies.append(
+            send(sum_core.at[q, 1 - pair], got_pair.at[q], pair_send.at[q], pair_recv.at[q], pair_mate)
+        )
+    far_copies = []
+    for q in range(PIECES):
+        pair_copies[q].wait()
+        value = sum_core[q, pair].astype(jnp.float32) + got_pair[q].astype(jnp.float32)
+        sum_pair[q] = value.astype(jnp.bfloat16)
+        far_copies.append([
+            send(
+                sum_pair.at[q, shift(far, d, groups)], got_far.at[q, d - 1],
+                far_send.at[q, d - 1], far_recv.at[q, d - 1], far_mate(d),
+            )
+            for d in range(1, groups)
+        ])
+    for copy in src_copies:
+        copy.wait()
+    value = prod_ref[t].astype(jnp.float32)
+    for d in range(1, teams):
+        value = value + got_src[d - 1].astype(jnp.float32)
+    src_ref[...] = value.astype(jnp.bfloat16)
+    lines = part_ref.shape[4]
+    for q in range(PIECES):
+        value = sum_pair[q, far].astype(jnp.float32)
+        for d in range(1, groups):
+            far_copies[q][d - 1].wait()
+            value = value + got_far[q, d - 1].astype(jnp.float32)
+        tgt_ref[q * lines : (q + 1) * lines] = value.astype(jnp.bfloat16)
+
+
+def exchange(product, part, devices, teams):
+    total, feat = product.shape
+    tile = total // teams
+    _, _, _, groups, lines, share, _ = part.shape
+    vmem = pl.BlockSpec(memory_space=pltpu.VMEM)
+    block = (groups, lines, share, feat)
+    dma = pltpu.SemaphoreType.DMA
+    return pl.pallas_call(
+        lambda *refs: exchange_kernel(devices, teams, *refs),
+        out_shape=(
+            jax.ShapeDtypeStruct((tile, feat), jnp.bfloat16),
+            jax.ShapeDtypeStruct((PIECES * lines, share, feat), jnp.bfloat16),
+        ),
+        in_specs=[vmem] * 2,
+        out_specs=(vmem, vmem),
+        scratch_shapes=[
+            pltpu.VMEM((PIECES, 2) + block, jnp.bfloat16),
+            pltpu.VMEM((PIECES,) + block, jnp.bfloat16),
+            pltpu.VMEM((PIECES,) + block, jnp.bfloat16),
+            pltpu.VMEM((teams, tile, feat), jnp.bfloat16),
+            pltpu.VMEM((PIECES, 2) + block, jnp.bfloat16),
+            pltpu.VMEM((PIECES,) + block, jnp.bfloat16),
+            dma((PIECES,)), dma((PIECES,)), dma((PIECES,)), dma((PIECES,)),
+            dma((PIECES, groups)), dma((PIECES, groups)),
+            dma((teams,)), dma((teams,)),
+        ],
+        compiler_params=pltpu.CompilerParams(
+            collective_id=0, has_side_effects=True, vmem_limit_bytes=32 * 2**20
+        ),
+    )(product.reshape(teams, tile, feat), part)
+
+
+def total_kernel(
+    teams, count, term_ref, out_ref, got_core, got_far, held, full,
+    core_send, core_recv, far_send, far_recv, all_send, all_recv, last_send, last_recv,
+):
+    s = lax.axis_index("src")
+    t = lax.axis_index("tgt")
+    size = term_ref.shape[1]
+    core = lax.rem(s, 2)
+    me = (s // 2) * teams + t
+    mate = (s + 1 - 2 * core, t)
+
+    def place(rank):
+        return (rank // teams * 2 + core, lax.rem(rank, teams))
+
+    barrier = pltpu.get_barrier_semaphore()
+    pl.semaphore_signal(barrier, inc=1, device_id=mate, device_id_type=MESH)
+
+    @pl.loop(1, size)
+    def _(d):
+        pl.semaphore_signal(
+            barrier, inc=1, device_id=place(shift(me, d, size)), device_id_type=MESH
+        )
+
+    pl.semaphore_wait(barrier, size)
+
+    def remote(src, dst, send_sem, recv_sem, device):
+        return pltpu.make_async_remote_copy(
+            src_ref=src, dst_ref=dst, send_sem=send_sem, recv_sem=recv_sem,
+            device_id=device, device_id_type=MESH,
+        )
+
+    copy = remote(term_ref.at[1 - core], got_core, core_send, core_recv, mate)
+    copy.start()
+    copy.wait()
+    value = term_ref[core].astype(jnp.float32) + got_core[...].astype(jnp.float32)
+    held[...] = value.astype(jnp.bfloat16)
+
+    def far_copy(d):
+        rank = shift(me, d, size)
+        return remote(
+            held.at[rank], got_far.at[d - 1], far_send.at[d - 1], far_recv.at[d - 1], place(rank)
+        )
+
+    @pl.loop(1, size)
+    def _(d):
+        far_copy(d).start()
+
+    def add(d, value):
+        far_copy(d).wait()
+        return value + got_far[d - 1].astype(jnp.float32)
+
+    value = lax.fori_loop(1, size, add, held[me].astype(jnp.float32))
+    full[core, me] = value.astype(jnp.bfloat16)
+
+    def all_copy(d, rank):
+        return remote(
+            full.at[core, rank], full.at[core, rank],
+            all_send.at[d - 1], all_recv.at[d - 1], place(shift(me, d, size)),
+        )
+
+    @pl.loop(1, size)
+    def _(d):
+        all_copy(d, me).start()
+
+    @pl.loop(1, size)
+    def _(d):
+        all_copy(d, me).wait_send()
+        all_copy(d, shift(me, size - d, size)).wait_recv()
+
+    remote(full.at[core], full.at[core], last_send, last_recv, mate).start()
+    remote(full.at[core], full.at[core], last_send, last_recv, mate).wait_send()
+    remote(full.at[1 - core], full.at[1 - core], last_send, last_recv, mate).wait_recv()
+    out_ref[...] = full[...].astype(jnp.float32) * (1.0 / count)
+
+
+def weight_totals(out_term, conv_term, devices, teams, count):
+    size = devices * teams // 2
+    flat = jnp.concatenate([out_term.reshape(-1, 128), conv_term.reshape(-1, 128)], axis=0)
+    flat = flat.astype(jnp.bfloat16)
+    used = flat.shape[0]
+    lines = -(-used // (2 * size * 16)) * 16
+    flat = jnp.pad(flat, ((0, 2 * size * lines - used), (0, 0)))
+    vmem = pl.BlockSpec(memory_space=pltpu.VMEM)
+    dma = pltpu.SemaphoreType.DMA
+    full = pl.pallas_call(
+        lambda *refs: total_kernel(teams, count, *refs),
+        out_shape=jax.ShapeDtypeStruct((2, size, lines, 128), jnp.float32),
+        in_specs=[vmem],
+        out_specs=vmem,
+        scratch_shapes=[
+            pltpu.VMEM((size, lines, 128), jnp.bfloat16),
+            pltpu.VMEM((size, lines, 128), jnp.bfloat16),
+            pltpu.VMEM((size, lines, 128), jnp.bfloat16),
+            pltpu.VMEM((2, size, lines, 128), jnp.bfloat16),
+            dma, dma, dma((size,)), dma((size,)), dma((size,)), dma((size,)), dma, dma,
+        ],
+        compiler_params=pltpu.CompilerParams(
+            collective_id=1, has_side_effects=True, vmem_limit_bytes=32 * 2**20
+        ),
+    )(flat.reshape(2, size, lines, 128))
+    full = full.reshape(-1, 128)
+    split = out_term.size // 128
+    return (
+        full[:split].reshape(out_term.shape),
+        full[split:used].reshape(conv_term.shape),
+    )
+
+
 def padded_2(array, sides, width):
     for axis, dim in sides:
         devices, length = (lax.axis_size(axis), array.shape[dim])
@@ -211,24 +443,19 @@
     feat_width = target_feats.shape[2]
     src_devices = lax.axis_size("src")
     tgt_devices = lax.axis_size("tgt")
-    product, target = corr_grads(upstream, centers, post_relu, target_feats, out_weight)
-    target_share = lax.psum_scatter(target, "src", scatter_dimension=1, tiled=True)
-    tgt_grad = target_share.astype(jnp.bfloat16)
+    product, part = corr_grads(
+        upstream, centers, post_relu, target_feats, out_weight, src_devices
+    )
+    src_grad, tgt_grad = exchange(product, part, src_devices, tgt_devices)
     tile_rows = src_rows // tgt_devices
-    src_grad = lax.psum_scatter(
-        product.reshape(src_rows, src_width, feat_width),
-        "tgt",
-        scatter_dimension=0,
-        tiled=True,
-    ).astype(jnp.bfloat16)
+    src_grad = src_grad.reshape(tile_rows, src_width, feat_width)
     relu_tile = lax.dynamic_slice_in_dim(post_relu, lax.axis_index("tgt") * tile_rows, tile_rows, 0)
     block_grad, out_term = hidden_grads(src_grad, relu_tile, out_weight)
     grad_pad = padded_2(block_grad, ((("src", "tgt"), 0),), 1)
     act_sum, conv_term = conv_back(grad_pad, conv_input, conv_weight)
-    out_total, conv_total = lax.psum((out_term, conv_term), ("src", "tgt"))
-    act_grad = act_sum.astype(jnp.bfloat16)
     row_count = float(src_rows * src_devices)
-    return (tgt_grad, act_grad, out_total / row_count, conv_total / row_count)
+    out_total, conv_total = weight_totals(out_term, conv_term, src_devices, tgt_devices, row_count)
+    return (tgt_grad, act_sum.astype(jnp.bfloat16), out_total, conv_total)
 
 
 def solution(mesh):

time: 218 us -> 77.8 us (0.36)
  waiting for transfers between devices: 155 us -> 1.3 us
  Pallas kernels: 21.9 us -> 59.7 us
  between operations: 15.7 us -> 0.92 us
  other arithmetic: 5.1 us -> 0.09 us
  matrix products: 7.59 us -> 4.97 us
    psum x1 -> x0, waiting for transfers between devices: 132 us -> none  [body(): out_total, conv_total = lax.psum((out_term, conv_term), ('src', 'tgt'))]
    pallas_call x0 -> x2, Pallas kernels: none -> 39.1 us  [the longest x1 20.6 us: weight_totals(): pl.pallas_call(lambda *refs: total_kernel(teams, count, *refs), out_shape...]
    reduce_scatter x2 -> x0, waiting for transfers between devices: 23.1 us -> none  [the longest x1 23.1 us: body(): lax.psum_scatter(product.reshape(src_rows, src_width, feat_width), 'tgt',...]
    div x2 -> x0, other arithmetic: 3.49 us -> none  [body(): return (tgt_grad, act_grad, out_total / row_count, conv_total / row_count)]
    unnamed x17 -> x14, local copies, waits for them, and re-layouts: 5.31 us -> 3.12 us
  transfers between devices with their start and end apart: 5 -> 2, of which waited for: 2 -> 1; matrix products, arithmetic and copies ran while one was open for 4% -> 0% of each run, Pallas kernels for 0% -> 0%
where the time goes in v2:
time: 77.8 us; the launch traced here: 77.5 us
  Pallas kernels  59.7 us (77%)
  starting transfers between devices  5.84 us (8%)
  matrix products  4.97 us (6%)
  local copies, waits for them, and re-layouts  4.71 us (6%)
  waiting for transfers between devices  1.3 us (2%)
  between operations  0.92 us (1%)
    pallas_call x1, Pallas kernels, weight_totals(): pl.pallas_call(lambda *refs: total_kernel(teams, count, *refs), out_shape...  20.6 us
    pallas_call x1, Pallas kernels, corr_grads(): pl.pallas_call(corr_kernel, out_shape=(jax.ShapeDtypeStruct((total, feat)...  20.6 us
    pallas_call x1, Pallas kernels, exchange(): pl.pallas_call(lambda *refs: exchange_kernel(devices, teams, *refs), out_...  18.6 us
    ppermute x1, starting transfers between devices, padded_2(): before = lax.ppermute(last, axis, up)  4.55 us
    unnamed x14, local copies, waits for them, and re-layouts  3.12 us
    dot_general x9, matrix products, conv_back(): jnp.einsum('rwo,io->rwi', window, kernel[row_tap, col_tap], preferred_ele...  2.32 us
    dot_general x9, matrix products, conv_back(): jnp.einsum('rwi,rwo->io', inputs, window, preferred_element_type=jnp.floa...  2.18 us
  transfers between devices with their start and end apart: 2, of which 1 were waited for; matrix products, arithmetic and copies ran while one was open for 0% of the time, Pallas kernels for 0%

profile of v2, /device:TPU:0, one launch (start us, length us, event | category | flops | bytes accessed | tf_op | source)
XLA Modules:
  0.0 77.5 jit_solution(7510778061698304749)
XLA Ops:
  0.6 0.0 copy-start
  0.6 0.0 copy-start.3
  0.7 0.0 copy-start.1
  0.7 0.0 copy-start.2
  0.7 1.7 %copy.11 = bf16[8,128,324]{2,1,0:T(8,128)(2,1)S(1)} copy(bf16[8,128,324]{1,0,2:T(8,128)(2,1)} %param.7) | data formatting | bytes 1327104 | tf_op args[0]
  2.3 0.0 copy-start.4
  2.4 0.0 copy-done.3
  2.4 0.0 copy-done.1
  2.4 0.0 copy-done.2
  2.4 0.7 copy-done.4
  3.0 20.6 %shard_map.102 = (bf16[1024,256]{1,0:T(8,128)(2,1)S(1)}, bf16[2,2,2,4,4,16,256]{6,5,4,3,2,1,0:T(8,128)(2,1)S(1)}) custom-call(bf16[1024,324]{1,0:T(8,128)(2,1)S(1)} %bitcast.204, s32[2,8,128]{2,1,0:T(8,128)S(1)} %copy-done.4, bf16[1024,128]{1,0:T(8,128)(2,1)S(1)} %bitcast.206, bf16[8,256,256]{2,1,0:T(8,128)(2,1)S(1)} %copy-done.3, bf16[128,256]{1,0:T(8,128)(2,1)S(1)} %copy-done.2), custom_call_target="tpu_custom_call" | custom-call | flops 2952790016 | bytes 6291456 | tf_op jit(solution)/shard_map/pallas_call | solution.py:145
  23.6 18.6 %shard_map.103 = (bf16[512,256]{1,0:T(8,128)(2,1)S(1)}, bf16[8,16,256]{2,1,0:T(8,128)(2,1)S(1)}) custom-call(bf16[2,512,256]{2,1,0:T(8,128)(2,1)S(1)} %bitcast.205, bf16[2,2,2,4,4,16,256]{6,5,4,3,2,1,0:T(8,128)(2,1)S(1)} %get-tuple-element.9.refs_1_), custom_call_target="tpu_custom_call" | custom-call | tf_op jit(solution)/shard_map/pallas_call | solution.py:267
  42.2 0.2 fusion.1
  42.4 1.3 %collective-permute-start.1 = (bf16[1,128,128]{2,1,0:T(8,128)(2,1)S(1)}, bf16[1,128,128]{2,1,0:T(8,128)(2,1)S(1)}, u32[]{:S(2)}, u32[]{:S(2)}) collective-permute-start(bf16[1,128,128]{2,1,0:T(8,128)(2,1)S(1)} %get-tuple-element.13), channel_id=1, source_target_pairs={{1,0},{2,1},{3,2},{4,3},{5,4},{6,5},{7,6},{8,7},{9,8},{10,9},{11,1... | collective-permute-start | bytes 98312 | tf_op jit(solution)/shard_map/ppermute | solution.py:408
  43.7 4.5 %collective-permute-start = (bf16[1,128,128]{2,1,0:T(8,128)(2,1)S(1)}, bf16[1,128,128]{2,1,0:T(8,128)(2,1)S(1)}, u32[]{:S(2)}, u32[]{:S(2)}) collective-permute-start(bf16[1,128,128]{2,1,0:T(8,128)(2,1)S(1)} %get-tuple-element.12), channel_id=1, source_target_pairs={{0,1},{1,2},{2,3},{3,4},{4,5},{5,6},{6,7},{7,8},{8,9},{9,10},{10,1... | collective-permute-start | bytes 98312 | tf_op jit(solution)/shard_map/ppermute | solution.py:407
  48.3 0.2 fusion.3
  48.6 0.0 collective-permute-done.1
  48.6 1.3 %collective-permute-done = bf16[1,128,128]{2,1,0:T(8,128)(2,1)S(1)} collective-permute-done((bf16[1,128,128]{2,1,0:T(8,128)(2,1)S(1)}, bf16[1,128,128]{2,1,0:T(8,128)(2,1)S(1)}, u32[]{:S(2)}, u32[]{:S(2)}) %collective-permute-start) | collective-permute-done | bytes 32800 | tf_op jit(solution)/shard_map/ppermute | solution.py:407
  49.9 0.1 fusion.39
  49.9 0.0 copy-done
  50.0 0.2 fusion.30
  50.2 0.2 fusion.16
  50.4 0.2 fusion.28
  50.7 0.2 fusion.26
  50.9 0.2 fusion.24
  51.2 0.2 fusion.22
  51.4 0.2 fusion.20
  51.7 0.2 fusion.14
  51.9 0.2 fusion.18
  52.2 20.6 %shard_map.104 = f32[2,16,48,128]{3,2,1,0:T(8,128)S(1)} custom-call(bf16[2,16,48,128]{3,2,1,0:T(8,128)(2,1)S(1)} %bitcast.201), custom_call_target="tpu_custom_call" | custom-call | tf_op jit(solution)/shard_map/pallas_call | solution.py:376
  72.8 0.0 copy-start.5
  72.8 0.9 %slice.99 = f32[1152,128]{1,0:T(8,128)} slice(f32[1536,128]{1,0:T(8,128)S(1)} %bitcast.200), slice={[256:1408], [0:128]} | slice | bytes 1179648 | tf_op jit(solution)/shard_map/slice | solution.py:396
  73.7 0.1 copy-done.5
  73.8 0.2 fusion.41
  74.0 0.2 fusion.54
  74.2 0.2 convolution_add_fusion.6
  74.4 0.2 convolution_add_fusion.5
  74.6 0.2 convolution_add_fusion.4
  74.8 0.2 convolution_add_fusion.3
  75.0 0.2 convolution_add_fusion.2
  75.2 0.2 convolution_add_fusion.1
  75.3 0.7 reshape.43
  76.0 0.8 %fusion.2 = bf16[4,128,128]{2,1,0:T(8,128)(2,1)} fusion(f32[4,128,128]{2,1,0:T(8,128)S(1)} %fusion.41, f32[4,128,128]{2,1,0:T(8,128)S(1)} %convolution_add_fusion.1, bf16[4,128,128]{2,1,0:T(8,128)(2,1)S(1)} %fusion.1, bf16[1,128,128]{2,1,0:T(8,128)(2,1)S(1)} %collective-permute-done, bf16[3,3,128,128]{3,2,1,0:T(8,128)(2,1)S(1)} %copy-done.5), kind=kOutput, calls=%fused_computation.10 | convolution fusion | flops 17301504 | bytes 851968 | tf_op jit(solution)/shard_map/rwo,io->rwi/dot_general | solution.py:431
  76.9 0.6 copy.41
  (4 shorter events, 0.1 us)
Async XLA Ops:
  0.6 49.3 %copy-start = (bf16[4,128,128]{2,1,0:T(8,128)(2,1)S(1)}, bf16[4,128,128]{2,1,0:T(8,128)(2,1)}, u32[]{:S(2)}) copy-start(bf16[4,128,128]{2,1,0:T(8,128)(2,1)} %param.10) | copy-start | bytes 393220
  0.6 1.7 %copy-start.3 = (bf16[8,256,256]{2,1,0:T(8,128)(2,1)S(1)}, bf16[8,256,256]{2,1,0:T(8,128)(2,1)}, u32[]{:S(2)}) copy-start(bf16[8,256,256]{2,1,0:T(8,128)(2,1)} %tf_ref.1) | copy-start | bytes 3145732
  0.7 1.7 %copy-start.1 = (bf16[8,128,128]{2,1,0:T(8,128)(2,1)S(1)}, bf16[8,128,128]{2,1,0:T(8,128)(2,1)}, u32[]{:S(2)}) copy-start(bf16[8,128,128]{2,1,0:T(8,128)(2,1)} %param.9) | copy-start | bytes 786436
  0.7 1.7 %copy-start.2 = (bf16[128,256]{1,0:T(8,128)(2,1)S(1)}, bf16[128,256]{1,0:T(8,128)(2,1)}, u32[]{:S(2)}) copy-start(bf16[128,256]{1,0:T(8,128)(2,1)} %ow_ref.1) | copy-start | bytes 196612
  2.3 0.7 copy-start.4
  42.4 6.1 %collective-permute-start.1 = (bf16[1,128,128]{2,1,0:T(8,128)(2,1)S(1)}, bf16[1,128,128]{2,1,0:T(8,128)(2,1)S(1)}, u32[]{:S(2)}, u32[]{:S(2)}) collective-permute-start(bf16[1,128,128]{2,1,0:T(8,128)(2,1)S(1)} %get-tuple-element.13), channel_id=1, source_target_pairs={{1,0},{2,1},{3,2},{4,3},{5,4},{6,5},{7,6},{8,7},{9,8},{10,9},{11,1... | collective-permute-start | bytes 98312 | tf_op jit(solution)/shard_map/ppermute | solution.py:408
  43.7 6.1 %collective-permute-start = (bf16[1,128,128]{2,1,0:T(8,128)(2,1)S(1)}, bf16[1,128,128]{2,1,0:T(8,128)(2,1)S(1)}, u32[]{:S(2)}, u32[]{:S(2)}) collective-permute-start(bf16[1,128,128]{2,1,0:T(8,128)(2,1)S(1)} %get-tuple-element.12), channel_id=1, source_target_pairs={{0,1},{1,2},{2,3},{3,4},{4,5},{5,6},{6,7},{7,8},{8,9},{9,10},{10,1... | collective-permute-start | bytes 98312 | tf_op jit(solution)/shard_map/ppermute | solution.py:407
  72.8 1.0 %copy-start.5 = (bf16[3,3,128,128]{3,2,1,0:T(8,128)(2,1)S(1)}, bf16[3,3,128,128]{3,2,1,0:T(8,128)(2,1)}, u32[]{:S(2)}) copy-start(bf16[3,3,128,128]{3,2,1,0:T(8,128)(2,1)} %param.13) | copy-start | bytes 884740

commit v3 on v1

--- a/solution.py
+++ b/solution.py
@@ -10,6 +10,8 @@
 OFFSET = (0, 81, 34, 115)
 EMPTY = (100, 178, 120, 208)
 FAR = 4096
+PIECES = 2
+MESH = pl.DeviceIdType.MESH
 
 
 def dot(a, b, dims=((1,), (0,))):
@@ -126,10 +128,15 @@
             mat[:, :128], sums_ref[:, dense + j * 128 : dense + (j + 1) * 128], ((1,), (1,))
         )
         value = value + dot(mat[:, 128:], sums_ref[:, dense + 512 :], ((1,), (1,)))
-        tgt_ref[y] = (value * scale).astype(tgt_ref.dtype)
-
-
-def corr_grads(upstream, centers, post_relu, target_feats, out_weight):
+        value = (value * scale).astype(tgt_ref.dtype)
+        pieces, _, _, groups, lines, share, _ = tgt_ref.shape
+        for k in range(4 * groups):
+            tgt_ref[y // lines, k % 2, k // 2 % 2, k // 4, y % lines] = value[
+                k * share : (k + 1) * share
+            ]
+
+
+def corr_grads(upstream, centers, post_relu, target_feats, out_weight, devices):
     total = upstream.shape[0] * upstream.shape[1]
     rows, width, feat = target_feats.shape
     assert rows == 8 and width == 256
@@ -138,8 +145,10 @@
     return pl.pallas_call(
         corr_kernel,
         out_shape=(
-            jax.ShapeDtypeStruct((total, feat), jnp.float32),
-            jax.ShapeDtypeStruct((rows, width, feat), jnp.float32),
+            jax.ShapeDtypeStruct((total, feat), jnp.bfloat16),
+            jax.ShapeDtypeStruct(
+                (PIECES, 2, 2, devices // 4, rows // PIECES, width // devices, feat), jnp.bfloat16
+            ),
         ),
         in_specs=[vmem] * 5,
         out_specs=(vmem, vmem),
@@ -165,70 +174,308 @@
     )
 
 
-def padded_2(array, sides, width):
-    for axis, dim in sides:
-        devices, length = (lax.axis_size(axis), array.shape[dim])
-        up = [(i, (i + 1) % devices) for i in range(devices - 1)]
-        down = [(j, i) for i, j in up]
-        last = lax.slice_in_dim(array, length - width, length, axis=dim)
-        first = lax.slice_in_dim(array, 0, width, axis=dim)
-        before = lax.ppermute(last, axis, up)
-        after = lax.ppermute(first, axis, down)
-        array = jnp.concatenate([before, array, after], axis=dim)
-    return array
-
-
-def hidden_grads(src_grad, relu_rows, out_weight):
-    hidden = jnp.einsum("rwd,cd->rwc", src_grad, out_weight, preferred_element_type=jnp.float32)
-    block_grad = jnp.where(relu_rows > 0, hidden, 0.0).astype(jnp.bfloat16)
-    out_term = jnp.einsum("rwc,rwd->cd", relu_rows, src_grad, preferred_element_type=jnp.float32)
-    return (block_grad, out_term)
-
-
-def conv_back(grad_pad, inputs, kernel):
-    row_total = inputs.shape[0]
-    width_total = inputs.shape[1]
-    padded = jnp.pad(grad_pad, ((0, 0), (1, 1), (0, 0)))
-    act_sum = jnp.zeros(inputs.shape, jnp.float32)
-    tap_grads = []
-    for row_tap in range(3):
-        for col_tap in range(3):
-            window = padded[
-                2 - row_tap : 2 - row_tap + row_total, 2 - col_tap : 2 - col_tap + width_total
-            ]
-            act_sum = act_sum + jnp.einsum(
-                "rwo,io->rwi", window, kernel[row_tap, col_tap], preferred_element_type=jnp.float32
+def shift(value, step, size):
+    return lax.rem(value + step, size)
+
+
+def tail_kernel(
+    devices, teams, count,
+    prod_ref, part_ref, relu_ref, input_ref, weight_ref, conv_ref,
+    tgt_ref, act_ref, out_ref, taps_ref,
+    got_core, got_pair, got_far, got_src, sum_core, sum_pair,
+    edge, got_edge, padded, window, terms, got_half, held, got_rest, full,
+    core_send, core_recv, pair_send, pair_recv, far_send, far_recv, src_send, src_recv,
+    edge_send, edge_recv, half_send, half_recv, rest_send, rest_recv,
+    all_send, all_recv, last_send, last_recv,
+):
+    s = lax.axis_index("src")
+    t = lax.axis_index("tgt")
+    groups = devices // 4
+    size = devices * teams // 2
+    tile, width, channels = input_ref.shape
+    lines = terms.shape[0] // (2 * size)
+    core, pair, far = lax.rem(s, 2), lax.rem(s // 2, 2), s // 4
+    me = (s // 2) * teams + t
+    spot = s * teams + t
+    core_mate = (s + 1 - 2 * core, t)
+    pair_mate = (s + 2 - 4 * pair, t)
+
+    def far_mate(d):
+        return (shift(far, d, groups) * 4 + pair * 2 + core, t)
+
+    def place(rank):
+        return (rank // teams * 2 + core, lax.rem(rank, teams))
+
+    everyone = devices * teams
+    up, down = shift(spot, everyone - 1, everyone), shift(spot, 1, everyone)
+    above = (up // teams, lax.rem(up, teams))
+    below = (down // teams, lax.rem(down, teams))
+    has_above = spot > 0
+    has_below = spot < devices * teams - 1
+
+    barrier = pltpu.get_barrier_semaphore()
+    pl.semaphore_signal(barrier, inc=1, device_id=core_mate, device_id_type=MESH)
+
+    @pl.loop(1, size)
+    def _(d):
+        pl.semaphore_signal(
+            barrier, inc=1, device_id=place(shift(me, d, size)), device_id_type=MESH
+        )
+
+    for device in (above, below):
+        pl.semaphore_signal(barrier, inc=1, device_id=device, device_id_type=MESH)
+    pl.semaphore_wait(barrier, size + 2)
+
+    def remote(src, dst, send_sem, recv_sem, device):
+        return pltpu.make_async_remote_copy(
+            src_ref=src, dst_ref=dst, send_sem=send_sem, recv_sem=recv_sem,
+            device_id=device, device_id_type=MESH,
+        )
+
+    def send(*args):
+        copy = remote(*args)
+        copy.start()
+        return copy
+
+    core_copies = [
+        send(part_ref.at[q, 1 - core], got_core.at[q], core_send.at[q], core_recv.at[q], core_mate)
+        for q in range(PIECES)
+    ]
+    src_copies = [
+        send(
+            prod_ref.at[shift(t, d, teams)], got_src.at[d - 1],
+            src_send.at[d - 1], src_recv.at[d - 1], (s, shift(t, d, teams)),
+        )
+        for d in range(1, teams)
+    ]
+    pair_copies = []
+    for q in range(PIECES):
+        core_copies[q].wait()
+        for half in range(2):
+            value = part_ref[q, core, half].astype(jnp.float32)
+            value = value + got_core[q, half].astype(jnp.float32)
+            sum_core[q, half] = value.astype(jnp.bfloat16)
+        pair_copies.append(
+            send(sum_core.at[q, 1 - pair], got_pair.at[q], pair_send.at[q], pair_recv.at[q], pair_mate)
+        )
+    far_copies = []
+
+    def far_step(q):
+        pair_copies[q].wait()
+        value = sum_core[q, pair].astype(jnp.float32) + got_pair[q].astype(jnp.float32)
+        sum_pair[q] = value.astype(jnp.bfloat16)
+        far_copies.append([
+            send(
+                sum_pair.at[q, shift(far, d, groups)], got_far.at[q, d - 1],
+                far_send.at[q, d - 1], far_recv.at[q, d - 1], far_mate(d),
             )
-            tap_grads.append(
-                jnp.einsum("rwi,rwo->io", inputs, window, preferred_element_type=jnp.float32)
-            )
-    channels = inputs.shape[2]
-    return (act_sum, jnp.stack(tap_grads).reshape(3, 3, channels, channels))
+            for d in range(1, groups)
+        ])
+
+    far_step(0)
+    value = prod_ref[t].astype(jnp.float32)
+    for d in range(1, teams):
+        src_copies[d - 1].wait()
+        value = value + got_src[d - 1].astype(jnp.float32)
+    src_grad = value.astype(jnp.bfloat16)
+    relu = relu_ref[pl.ds(t * tile, tile)].reshape(tile * width, channels)
+    hidden = dot(src_grad, weight_ref[...], ((1,), (1,)))
+    hidden = jnp.where(relu.astype(jnp.float32) > 0, hidden, 0.0)
+    rounded = hidden.astype(jnp.bfloat16)
+    edge[0] = rounded[:width]
+    edge[1] = rounded[(tile - 1) * width :]
+
+    def up_copy():
+        return remote(edge.at[0], got_edge.at[1], edge_send.at[0], edge_recv.at[1], above)
+
+    def down_copy():
+        return remote(edge.at[1], got_edge.at[0], edge_send.at[1], edge_recv.at[0], below)
+
+    @pl.when(has_above)
+    def _():
+        up_copy().start()
+
+    @pl.when(has_below)
+    def _():
+        down_copy().start()
+
+    padded[width : (tile + 1) * width] = rounded.astype(jnp.float32)
+    out_term = dot(relu, src_grad, ((0,), (0,))).astype(jnp.bfloat16)
+    for half in range(2):
+        terms[half * channels : (half + 1) * channels] = out_term[:, half * 128 : (half + 1) * 128]
+    for q in range(1, PIECES):
+        far_step(q)
+
+    @pl.when(has_above)
+    def _():
+        up_copy().wait_send()
+        remote(edge.at[1], got_edge.at[0], edge_send.at[1], edge_recv.at[0], above).wait_recv()
+        padded[0:width] = got_edge[0].astype(jnp.float32)
+
+    @pl.when(jnp.logical_not(has_above))
+    def _():
+        padded[0:width] = jnp.zeros((width, channels), jnp.float32)
+
+    @pl.when(has_below)
+    def _():
+        down_copy().wait_send()
+        remote(edge.at[0], got_edge.at[1], edge_send.at[0], edge_recv.at[1], below).wait_recv()
+        padded[(tile + 1) * width :] = got_edge[1].astype(jnp.float32)
+
+    @pl.when(jnp.logical_not(has_below))
+    def _():
+        padded[(tile + 1) * width :] = jnp.zeros((width, channels), jnp.float32)
+
+    whole = padded[...]
+    total = whole.shape[0]
+    column = lax.rem(lax.broadcasted_iota(jnp.int32, whole.shape, 0), width)
+    right = jnp.where(column < width - 1, pltpu.roll(whole, total - 1, 0), 0.0)
+    left = jnp.where(column > 0, pltpu.roll(whole, 1, 0), 0.0)
+    for q, value in enumerate((right, whole, left)):
+        window[:, q * channels : (q + 1) * channels] = value.astype(jnp.bfloat16)
+    inputs = input_ref[...].reshape(tile * width, channels)
+    base = 2 * channels
+    for p in range(3):
+        rows = window[(2 - p) * width : (2 - p + tile) * width]
+        grads = dot(inputs, rows, ((0,), (0,))).astype(jnp.bfloat16)
+        for q in range(3):
+            first = base + (3 * p + q) * channels
+            terms[first : first + channels] = grads[:, q * channels : (q + 1) * channels]
+    used = base + 9 * channels
+    if used < terms.shape[0]:
+        terms[used:] = jnp.zeros((terms.shape[0] - used, 128), jnp.bfloat16)
+
+    def rows_of(half, first, number):
+        start = (half * size + first) * lines
+        return pl.ds(pl.multiple_of(start, 16), number * lines)
+
+    half_copy = send(terms.at[rows_of(1 - core, 0, size)], got_half, half_send, half_recv, core_mate)
+    act = jnp.zeros((tile * width, channels), jnp.float32)
+    for p in range(3):
+        rows = window[(2 - p) * width : (2 - p + tile) * width]
+        taps = jnp.concatenate([conv_ref[p, q] for q in range(3)], axis=1)
+        act = act + dot(rows, taps, ((1,), (1,)))
+    act_ref[...] = act.reshape(act_ref.shape).astype(act_ref.dtype)
+    half_copy.wait()
+    value = terms[rows_of(core, 0, size)].astype(jnp.float32) + got_half[...].astype(jnp.float32)
+    held[...] = value.astype(jnp.bfloat16)
+
+    def rest_copy(d):
+        rank = shift(me, d, size)
+        return remote(
+            held.at[rows_of(0, rank, 1)], got_rest.at[d - 1],
+            rest_send.at[d - 1], rest_recv.at[d - 1], place(rank),
+        )
+
+    @pl.loop(1, size)
+    def _(d):
+        rest_copy(d).start()
+
+    depth = part_ref.shape[4]
+    for q in range(PIECES):
+        value = sum_pair[q, far].astype(jnp.float32)
+        for d in range(1, groups):
+            far_copies[q][d - 1].wait()
+            value = value + got_far[q, d - 1].astype(jnp.float32)
+        tgt_ref[q * depth : (q + 1) * depth] = value.astype(jnp.bfloat16)
+
+    def add(d, value):
+        rest_copy(d).wait()
+        return value + got_rest[d - 1].astype(jnp.float32)
+
+    value = lax.fori_loop(1, size, add, held[rows_of(0, me, 1)].astype(jnp.float32))
+    full[rows_of(core, me, 1)] = value.astype(jnp.bfloat16)
+
+    def all_copy(d, rank):
+        rows = rows_of(core, rank, 1)
+        return remote(
+            full.at[rows], full.at[rows],
+            all_send.at[d - 1], all_recv.at[d - 1], place(shift(me, d, size)),
+        )
+
+    @pl.loop(1, size)
+    def _(d):
+        all_copy(d, me).start()
+
+    @pl.loop(1, size)
+    def _(d):
+        all_copy(d, me).wait_send()
+        all_copy(d, shift(me, size - d, size)).wait_recv()
+
+    mine = full.at[rows_of(core, 0, size)]
+    other = full.at[rows_of(1 - core, 0, size)]
+    remote(mine, mine, last_send, last_recv, core_mate).start()
+    remote(mine, mine, last_send, last_recv, core_mate).wait_send()
+    remote(other, other, last_send, last_recv, core_mate).wait_recv()
+    for half in range(2):
+        out_ref[:, half * 128 : (half + 1) * 128] = (
+            full[half * channels : (half + 1) * channels].astype(jnp.float32) * (1.0 / count)
+        )
+    taps_ref[...] = full[base:used].astype(jnp.float32) * (1.0 / count)
+
+
+def tail(product, part, post_relu, conv_input, out_weight, conv_weight, devices, teams):
+    total, feat = product.shape
+    share_rows = total // teams
+    _, _, _, groups, lines, share, _ = part.shape
+    tile, width, channels = conv_input.shape
+    assert channels == 128 and feat == 256
+    size = devices * teams // 2
+    used = 11 * channels
+    chunk = -(-used // (2 * size * 16)) * 16
+    count = float(post_relu.shape[0] * devices)
+    vmem = pl.BlockSpec(memory_space=pltpu.VMEM)
+    block = (groups, lines, share, feat)
+    dma = pltpu.SemaphoreType.DMA
+    bf16 = jnp.bfloat16
+    return pl.pallas_call(
+        lambda *refs: tail_kernel(devices, teams, count, *refs),
+        out_shape=(
+            jax.ShapeDtypeStruct((PIECES * lines, share, feat), bf16),
+            jax.ShapeDtypeStruct((tile, width, channels), bf16),
+            jax.ShapeDtypeStruct((channels, feat), jnp.float32),
+            jax.ShapeDtypeStruct((9 * channels, channels), jnp.float32),
+        ),
+        in_specs=[vmem] * 6,
+        out_specs=(vmem,) * 4,
+        scratch_shapes=[
+            pltpu.VMEM((PIECES, 2) + block, bf16),
+            pltpu.VMEM((PIECES,) + block, bf16),
+            pltpu.VMEM((PIECES,) + block, bf16),
+            pltpu.VMEM((teams, share_rows, feat), bf16),
+            pltpu.VMEM((PIECES, 2) + block, bf16),
+            pltpu.VMEM((PIECES,) + block, bf16),
+            pltpu.VMEM((2, width, channels), bf16),
+            pltpu.VMEM((2, width, channels), bf16),
+            pltpu.VMEM(((tile + 2) * width, channels), jnp.float32),
+            pltpu.VMEM(((tile + 2) * width, 3 * channels), bf16),
+            pltpu.VMEM((2 * size * chunk, 128), bf16),
+            pltpu.VMEM((size * chunk, 128), bf16),
+            pltpu.VMEM((size * chunk, 128), bf16),
+            pltpu.VMEM((size, chunk, 128), bf16),
+            pltpu.VMEM((2 * size * chunk, 128), bf16),
+            dma((PIECES,)), dma((PIECES,)), dma((PIECES,)), dma((PIECES,)),
+            dma((PIECES, groups)), dma((PIECES, groups)),
+            dma((teams,)), dma((teams,)),
+            dma((2,)), dma((2,)), dma, dma, dma((size,)), dma((size,)),
+            dma((size,)), dma((size,)), dma, dma,
+        ],
+        compiler_params=pltpu.CompilerParams(
+            collective_id=0, has_side_effects=True, vmem_limit_bytes=40 * 2**20
+        ),
+    )(
+        product.reshape(teams, share_rows, feat), part, post_relu, conv_input, out_weight, conv_weight
+    )
 
 
 def body(upstream, centers, post_relu, conv_input, target_feats, out_weight, conv_weight):
-    src_rows, src_width, lookups = upstream.shape
-    feat_width = target_feats.shape[2]
-    src_devices = lax.axis_size("src")
-    tgt_devices = lax.axis_size("tgt")
-    product, target = corr_grads(upstream, centers, post_relu, target_feats, out_weight)
-    target_share = lax.psum_scatter(target, "src", scatter_dimension=1, tiled=True)
-    tgt_grad = target_share.astype(jnp.bfloat16)
-    tile_rows = src_rows // tgt_devices
-    src_grad = lax.psum_scatter(
-        product.reshape(src_rows, src_width, feat_width),
-        "tgt",
-        scatter_dimension=0,
-        tiled=True,
-    ).astype(jnp.bfloat16)
-    relu_tile = lax.dynamic_slice_in_dim(post_relu, lax.axis_index("tgt") * tile_rows, tile_rows, 0)
-    block_grad, out_term = hidden_grads(src_grad, relu_tile, out_weight)
-    grad_pad = padded_2(block_grad, ((("src", "tgt"), 0),), 1)
-    act_sum, conv_term = conv_back(grad_pad, conv_input, conv_weight)
-    out_total, conv_total = lax.psum((out_term, conv_term), ("src", "tgt"))
-    act_grad = act_sum.astype(jnp.bfloat16)
-    row_count = float(src_rows * src_devices)
-    return (tgt_grad, act_grad, out_total / row_count, conv_total / row_count)
+    devices = lax.axis_size("src")
+    teams = lax.axis_size("tgt")
+    product, part = corr_grads(upstream, centers, post_relu, target_feats, out_weight, devices)
+    tgt_grad, act_grad, out_wgrad, taps = tail(
+        product, part, post_relu, conv_input, out_weight, conv_weight, devices, teams
+    )
+    return (tgt_grad, act_grad, out_wgrad, taps.reshape(conv_weight.shape))
 
 
 def solution(mesh):

time: 218 us -> 59.8 us (0.27)
  waiting for transfers between devices: 155 us -> 0 us
  Pallas kernels: 21.9 us -> 54.5 us
  between operations: 15.7 us -> 0.74 us
  matrix products: 7.59 us -> 0 us
  starting transfers between devices: 5.96 us -> 0 us
  other arithmetic: 5.1 us -> 0 us
    psum x1 -> x0, waiting for transfers between devices: 132 us -> none  [body(): out_total, conv_total = lax.psum((out_term, conv_term), ('src', 'tgt'))]
    pallas_call x0 -> x1, Pallas kernels: none -> 34 us  [tail(): pl.pallas_call(lambda *refs: tail_kernel(devices, teams, count, *refs), o...]
    reduce_scatter x2 -> x0, waiting for transfers between devices: 23.1 us -> none  [the longest x1 23.1 us: body(): lax.psum_scatter(product.reshape(src_rows, src_width, feat_width), 'tgt',...]
    dot_general x20 -> x0, matrix products: 7.59 us -> none  [the longest x9 2.34 us: conv_back(): jnp.einsum('rwo,io->rwi', window, kernel[row_tap, col_tap], preferred_ele...]
    ppermute x2 -> x0, starting transfers between devices: 5.84 us -> none  [the longest x1 4.55 us: padded_2(): before = lax.ppermute(last, axis, up)]
    div x2 -> x0, other arithmetic: 3.49 us -> none  [body(): return (tgt_grad, act_grad, out_total / row_count, conv_total / row_count)]
  transfers between devices with their start and end apart: 5 -> 0, of which waited for: 2 -> 0; matrix products, arithmetic and copies ran while one was open for 4% -> 0% of each run, Pallas kernels for 0% -> 0%
where the time goes in v3:
time: 59.8 us; the launch traced here: 59.7 us
  Pallas kernels  54.5 us (91%)
  local copies, waits for them, and re-layouts  4.44 us (7%)
  between operations  0.74 us (1%)
    pallas_call x1, Pallas kernels, tail(): pl.pallas_call(lambda *refs: tail_kernel(devices, teams, count, *refs), o...  34 us
    pallas_call x1, Pallas kernels, corr_grads(): pl.pallas_call(corr_kernel, out_shape=(jax.ShapeDtypeStruct((total, feat)...  20.6 us
    unnamed x17, local copies, waits for them, and re-layouts  4.44 us

profile of v3, /device:TPU:0, one launch (start us, length us, event | category | flops | bytes accessed | tf_op | source)
XLA Modules:
  0.0 59.7 jit_solution(17552165121260182209)
XLA Ops:
  0.6 0.0 copy-start.4
  0.6 0.0 copy-start.1
  0.7 0.0 copy-start.3
  0.7 0.0 copy-start.5
  0.7 1.6 %copy.11 = bf16[8,128,324]{2,1,0:T(8,128)(2,1)S(1)} copy(bf16[8,128,324]{1,0,2:T(8,128)(2,1)} %param.7) | data formatting | bytes 1327104 | tf_op args[0]
  2.3 0.0 copy-done.4
  2.3 0.0 copy-done.1
  2.3 0.0 copy-done.3
  2.4 0.0 copy-done.5
  2.4 0.0 copy-start
  2.4 0.0 copy-start.2
  2.4 20.6 %shard_map.102 = (bf16[1024,256]{1,0:T(8,128)(2,1)S(1)}, bf16[2,2,2,4,4,16,256]{6,5,4,3,2,1,0:T(8,128)(2,1)S(1)}) custom-call(bf16[1024,324]{1,0:T(8,128)(2,1)S(1)} %bitcast.4, s32[2,8,128]{2,1,0:T(8,128)S(1)} %copy-done.5, bf16[1024,128]{1,0:T(8,128)(2,1)S(1)} %bitcast.7, bf16[8,256,256]{2,1,0:T(8,128)(2,1)S(1)} %copy-done.4, bf16[128,256]{1,0:T(8,128)(2,1)S(1)} %copy-done.3), custom_call_target="tpu_custom_call" | custom-call | flops 2952790016 | bytes 6291456 | tf_op jit(solution)/shard_map/pallas_call | solution.py:145
  23.0 0.0 copy-done
  23.0 0.0 copy-done.2
  23.0 34.0 %shard_map.103 = (bf16[8,16,256]{2,1,0:T(8,128)(2,1)S(1)}, bf16[4,128,128]{2,1,0:T(8,128)(2,1)S(1)}, f32[128,256]{1,0:T(8,128)S(1)}, f32[1152,128]{1,0:T(8,128)S(1)}) custom-call(bf16[2,512,256]{2,1,0:T(8,128)(2,1)S(1)} %bitcast.6, bf16[2,2,2,4,4,16,256]{6,5,4,3,2,1,0:T(8,128)(2,1)S(1)} %get-tuple-element.11.refs_1_, bf16[8,128,128]{2,1,0:T(8,128)(2,1)S(1)} %copy-done.1, ...), custom_call_target="tpu_custom_call" | custom-call | tf_op jit(solution)/shard_map/pallas_call | solution.py:431
  56.9 0.6 %copy.16 = bf16[8,16,256]{2,1,0:T(8,128)(2,1)} copy(bf16[8,16,256]{2,1,0:T(8,128)(2,1)S(1)} %get-tuple-element.20) | data formatting | bytes 131072
  57.6 0.7 %copy.17 = bf16[4,128,128]{2,1,0:T(8,128)(2,1)} copy(bf16[4,128,128]{2,1,0:T(8,128)(2,1)S(1)} %get-tuple-element.21) | data formatting | bytes 262144
  58.2 0.7 %copy.18 = f32[128,256]{1,0:T(8,128)} copy(f32[128,256]{1,0:T(8,128)S(1)} %get-tuple-element.22) | data formatting | bytes 262144
  58.9 0.8 %copy.19 = f32[3,3,128,128]{3,2,1,0:T(8,128)} copy(f32[3,3,128,128]{3,2,1,0:T(8,128)S(1)} %bitcast.5) | data formatting | bytes 1179648
Async XLA Ops:
  0.6 1.7 %copy-start.4 = (bf16[8,256,256]{2,1,0:T(8,128)(2,1)S(1)}, bf16[8,256,256]{2,1,0:T(8,128)(2,1)}, u32[]{:S(2)}) copy-start(bf16[8,256,256]{2,1,0:T(8,128)(2,1)} %tf_ref.1) | copy-start | bytes 3145732
  0.6 1.7 %copy-start.1 = (bf16[8,128,128]{2,1,0:T(8,128)(2,1)S(1)}, bf16[8,128,128]{2,1,0:T(8,128)(2,1)}, u32[]{:S(2)}) copy-start(bf16[8,128,128]{2,1,0:T(8,128)(2,1)} %refs_2_.1) | copy-start | bytes 786436
  0.7 1.7 %copy-start.3 = (bf16[128,256]{1,0:T(8,128)(2,1)S(1)}, bf16[128,256]{1,0:T(8,128)(2,1)}, u32[]{:S(2)}) copy-start(bf16[128,256]{1,0:T(8,128)(2,1)} %refs_4_.1) | copy-start | bytes 196612
  0.7 1.7 %copy-start.5 = (s32[2,8,128]{2,1,0:T(8,128)S(1)}, s32[2,8,128]{2,1,0:T(8,128)}, u32[]{:S(2)}) copy-start(s32[2,8,128]{2,1,0:T(8,128)} %cen_ref.1) | copy-start | bytes 24580
  2.4 20.6 %copy-start = (bf16[3,3,128,128]{3,2,1,0:T(8,128)(2,1)S(1)}, bf16[3,3,128,128]{3,2,1,0:T(8,128)(2,1)}, u32[]{:S(2)}) copy-start(bf16[3,3,128,128]{3,2,1,0:T(8,128)(2,1)} %refs_5_.1) | copy-start | bytes 884740
  2.4 20.6 %copy-start.2 = (bf16[4,128,128]{2,1,0:T(8,128)(2,1)S(1)}, bf16[4,128,128]{2,1,0:T(8,128)(2,1)}, u32[]{:S(2)}) copy-start(bf16[4,128,128]{2,1,0:T(8,128)(2,1)} %refs_3_.1) | copy-start | bytes 393220

commit v4 on v3

--- a/solution.py
+++ b/solution.py
@@ -37,7 +37,7 @@
     tail_ref[:, 0:68] = up_ref[:, 256:324].astype(jnp.float32)
     lane = lax.broadcasted_iota(jnp.int32, (16, 128), 1)
 
-    @pl.loop(0, total // 16)
+    @pl.loop(0, total // 16, unroll=2)
     def _(group):
         here = pl.ds(pl.multiple_of(group * 16, 16), 16)
         first = up_ref[here, 0:128].astype(jnp.float32)
@@ -371,6 +371,24 @@
     def _(d):
         rest_copy(d).start()
 
+    def add(d, value):
+        rest_copy(d).wait()
+        return value + got_rest[d - 1].astype(jnp.float32)
+
+    value = lax.fori_loop(1, size, add, held[rows_of(0, me, 1)].astype(jnp.float32))
+    full[rows_of(core, me, 1)] = value.astype(jnp.bfloat16)
+
+    def all_copy(d, rank):
+        rows = rows_of(core, rank, 1)
+        return remote(
+            full.at[rows], full.at[rows],
+            all_send.at[d - 1], all_recv.at[d - 1], place(shift(me, d, size)),
+        )
+
+    @pl.loop(1, size)
+    def _(d):
+        all_copy(d, me).start()
+
     depth = part_ref.shape[4]
     for q in range(PIECES):
         value = sum_pair[q, far].astype(jnp.float32)
@@ -378,24 +396,6 @@
             far_copies[q][d - 1].wait()
             value = value + got_far[q, d - 1].astype(jnp.float32)
         tgt_ref[q * depth : (q + 1) * depth] = value.astype(jnp.bfloat16)
-
-    def add(d, value):
-        rest_copy(d).wait()
-        return value + got_rest[d - 1].astype(jnp.float32)
-
-    value = lax.fori_loop(1, size, add, held[rows_of(0, me, 1)].astype(jnp.float32))
-    full[rows_of(core, me, 1)] = value.astype(jnp.bfloat16)
-
-    def all_copy(d, rank):
-        rows = rows_of(core, rank, 1)
-        return remote(
-            full.at[rows], full.at[rows],
-            all_send.at[d - 1], all_recv.at[d - 1], place(shift(me, d, size)),
-        )
-
-    @pl.loop(1, size)
-    def _(d):
-        all_copy(d, me).start()
 
     @pl.loop(1, size)
     def _(d):

time: 59.8 us -> 57.3 us (0.958)
  Pallas kernels: 54.5 us -> 52 us
    pallas_call x1, Pallas kernels: 20.6 us -> 18 us  [corr_grads(): pl.pallas_call(corr_kernel, out_shape=(jax.ShapeDtypeStruct((total, feat)...]
where the time goes in v4:
time: 57.3 us; the launch traced here: 57.2 us
  Pallas kernels  52 us (91%)
  local copies, waits for them, and re-layouts  4.44 us (8%)
  between operations  0.74 us (1%)
    pallas_call x1, Pallas kernels, tail(): pl.pallas_call(lambda *refs: tail_kernel(devices, teams, count, *refs), o...  34 us
    pallas_call x1, Pallas kernels, corr_grads(): pl.pallas_call(corr_kernel, out_shape=(jax.ShapeDtypeStruct((total, feat)...  18 us
    unnamed x17, local copies, waits for them, and re-layouts  4.44 us

profile of v4, /device:TPU:0, one launch (start us, length us, event | category | flops | bytes accessed | tf_op | source)
XLA Modules:
  0.0 57.2 jit_solution(8489464689144800930)
XLA Ops:
  0.6 0.0 copy-start.4
  0.6 0.0 copy-start.1
  0.7 0.0 copy-start.3
  0.7 0.0 copy-start.5
  0.7 1.6 %copy.11 = bf16[8,128,324]{2,1,0:T(8,128)(2,1)S(1)} copy(bf16[8,128,324]{1,0,2:T(8,128)(2,1)} %param.7) | data formatting | bytes 1327104 | tf_op args[0]
  2.3 0.0 copy-done.4
  2.3 0.0 copy-done.1
  2.3 0.0 copy-done.3
  2.4 0.0 copy-done.5
  2.4 0.0 copy-start
  2.4 0.0 copy-start.2
  2.4 18.0 %shard_map.102 = (bf16[1024,256]{1,0:T(8,128)(2,1)S(1)}, bf16[2,2,2,4,4,16,256]{6,5,4,3,2,1,0:T(8,128)(2,1)S(1)}) custom-call(bf16[1024,324]{1,0:T(8,128)(2,1)S(1)} %bitcast.4, s32[2,8,128]{2,1,0:T(8,128)S(1)} %copy-done.5, bf16[1024,128]{1,0:T(8,128)(2,1)S(1)} %bitcast.7, bf16[8,256,256]{2,1,0:T(8,128)(2,1)S(1)} %copy-done.4, bf16[128,256]{1,0:T(8,128)(2,1)S(1)} %copy-done.3), custom_call_target="tpu_custom_call" | custom-call | flops 2952790016 | bytes 6291456 | tf_op jit(solution)/shard_map/pallas_call | solution.py:145
  20.4 0.0 copy-done
  20.4 0.0 copy-done.2
  20.5 34.0 %shard_map.103 = (bf16[8,16,256]{2,1,0:T(8,128)(2,1)S(1)}, bf16[4,128,128]{2,1,0:T(8,128)(2,1)S(1)}, f32[128,256]{1,0:T(8,128)S(1)}, f32[1152,128]{1,0:T(8,128)S(1)}) custom-call(bf16[2,512,256]{2,1,0:T(8,128)(2,1)S(1)} %bitcast.6, bf16[2,2,2,4,4,16,256]{6,5,4,3,2,1,0:T(8,128)(2,1)S(1)} %get-tuple-element.11.refs_1_, bf16[8,128,128]{2,1,0:T(8,128)(2,1)S(1)} %copy-done.1, ...), custom_call_target="tpu_custom_call" | custom-call | tf_op jit(solution)/shard_map/pallas_call | solution.py:431
  54.4 0.6 %copy.16 = bf16[8,16,256]{2,1,0:T(8,128)(2,1)} copy(bf16[8,16,256]{2,1,0:T(8,128)(2,1)S(1)} %get-tuple-element.20) | data formatting | bytes 131072
  55.1 0.7 %copy.17 = bf16[4,128,128]{2,1,0:T(8,128)(2,1)} copy(bf16[4,128,128]{2,1,0:T(8,128)(2,1)S(1)} %get-tuple-element.21) | data formatting | bytes 262144
  55.7 0.7 %copy.18 = f32[128,256]{1,0:T(8,128)} copy(f32[128,256]{1,0:T(8,128)S(1)} %get-tuple-element.22) | data formatting | bytes 262144
  56.4 0.8 %copy.19 = f32[3,3,128,128]{3,2,1,0:T(8,128)} copy(f32[3,3,128,128]{3,2,1,0:T(8,128)S(1)} %bitcast.5) | data formatting | bytes 1179648
Async XLA Ops:
  0.6 1.7 %copy-start.4 = (bf16[8,256,256]{2,1,0:T(8,128)(2,1)S(1)}, bf16[8,256,256]{2,1,0:T(8,128)(2,1)}, u32[]{:S(2)}) copy-start(bf16[8,256,256]{2,1,0:T(8,128)(2,1)} %tf_ref.1) | copy-start | bytes 3145732
  0.6 1.7 %copy-start.1 = (bf16[8,128,128]{2,1,0:T(8,128)(2,1)S(1)}, bf16[8,128,128]{2,1,0:T(8,128)(2,1)}, u32[]{:S(2)}) copy-start(bf16[8,128,128]{2,1,0:T(8,128)(2,1)} %refs_2_.1) | copy-start | bytes 786436
  0.7 1.7 %copy-start.3 = (bf16[128,256]{1,0:T(8,128)(2,1)S(1)}, bf16[128,256]{1,0:T(8,128)(2,1)}, u32[]{:S(2)}) copy-start(bf16[128,256]{1,0:T(8,128)(2,1)} %refs_4_.1) | copy-start | bytes 196612
  0.7 1.7 %copy-start.5 = (s32[2,8,128]{2,1,0:T(8,128)S(1)}, s32[2,8,128]{2,1,0:T(8,128)}, u32[]{:S(2)}) copy-start(s32[2,8,128]{2,1,0:T(8,128)} %cen_ref.1) | copy-start | bytes 24580
  2.4 18.1 %copy-start = (bf16[3,3,128,128]{3,2,1,0:T(8,128)(2,1)S(1)}, bf16[3,3,128,128]{3,2,1,0:T(8,128)(2,1)}, u32[]{:S(2)}) copy-start(bf16[3,3,128,128]{3,2,1,0:T(8,128)(2,1)} %refs_5_.1) | copy-start | bytes 884740
  2.4 18.1 %copy-start.2 = (bf16[4,128,128]{2,1,0:T(8,128)(2,1)S(1)}, bf16[4,128,128]{2,1,0:T(8,128)(2,1)}, u32[]{:S(2)}) copy-start(bf16[4,128,128]{2,1,0:T(8,128)(2,1)} %refs_3_.1) | copy-start | bytes 393220

commit v5 on v4

--- a/solution.py
+++ b/solution.py
@@ -37,7 +37,7 @@
     tail_ref[:, 0:68] = up_ref[:, 256:324].astype(jnp.float32)
     lane = lax.broadcasted_iota(jnp.int32, (16, 128), 1)
 
-    @pl.loop(0, total // 16, unroll=2)
+    @pl.loop(0, total // 16, unroll=4)
     def _(group):
         here = pl.ds(pl.multiple_of(group * 16, 16), 16)
         first = up_ref[here, 0:128].astype(jnp.float32)

time: 57.3 us -> 56.2 us (0.981)
  Pallas kernels: 52 us -> 50.8 us
    pallas_call x1, Pallas kernels: 18 us -> 16.9 us  [corr_grads(): pl.pallas_call(corr_kernel, out_shape=(jax.ShapeDtypeStruct((total, feat)...]
where the time goes in v5:
time: 56.2 us; the launch traced here: 56 us
  Pallas kernels  50.8 us (90%)
  local copies, waits for them, and re-layouts  4.44 us (8%)
  between operations  0.74 us (1%)
    pallas_call x1, Pallas kernels, tail(): pl.pallas_call(lambda *refs: tail_kernel(devices, teams, count, *refs), o...  34 us
    pallas_call x1, Pallas kernels, corr_grads(): pl.pallas_call(corr_kernel, out_shape=(jax.ShapeDtypeStruct((total, feat)...  16.9 us
    unnamed x17, local copies, waits for them, and re-layouts  4.44 us

profile of v5, /device:TPU:0, one launch (start us, length us, event | category | flops | bytes accessed | tf_op | source)
XLA Modules:
  0.0 56.0 jit_solution(4067612533833574957)
XLA Ops:
  0.6 0.0 copy-start.4
  0.6 0.0 copy-start.1
  0.7 0.0 copy-start.3
  0.7 0.0 copy-start.5
  0.7 1.6 %copy.11 = bf16[8,128,324]{2,1,0:T(8,128)(2,1)S(1)} copy(bf16[8,128,324]{1,0,2:T(8,128)(2,1)} %param.7) | data formatting | bytes 1327104 | tf_op args[0]
  2.3 0.0 copy-done.4
  2.3 0.0 copy-done.1
  2.3 0.0 copy-done.3
  2.4 0.0 copy-done.5
  2.4 0.0 copy-start
  2.4 0.0 copy-start.2
  2.4 16.9 %shard_map.102 = (bf16[1024,256]{1,0:T(8,128)(2,1)S(1)}, bf16[2,2,2,4,4,16,256]{6,5,4,3,2,1,0:T(8,128)(2,1)S(1)}) custom-call(bf16[1024,324]{1,0:T(8,128)(2,1)S(1)} %bitcast.4, s32[2,8,128]{2,1,0:T(8,128)S(1)} %copy-done.5, bf16[1024,128]{1,0:T(8,128)(2,1)S(1)} %bitcast.7, bf16[8,256,256]{2,1,0:T(8,128)(2,1)S(1)} %copy-done.4, bf16[128,256]{1,0:T(8,128)(2,1)S(1)} %copy-done.3), custom_call_target="tpu_custom_call" | custom-call | flops 2952790016 | bytes 6291456 | tf_op jit(solution)/shard_map/pallas_call | solution.py:145
  19.3 0.0 copy-done
  19.3 0.0 copy-done.2
  19.3 34.0 %shard_map.103 = (bf16[8,16,256]{2,1,0:T(8,128)(2,1)S(1)}, bf16[4,128,128]{2,1,0:T(8,128)(2,1)S(1)}, f32[128,256]{1,0:T(8,128)S(1)}, f32[1152,128]{1,0:T(8,128)S(1)}) custom-call(bf16[2,512,256]{2,1,0:T(8,128)(2,1)S(1)} %bitcast.6, bf16[2,2,2,4,4,16,256]{6,5,4,3,2,1,0:T(8,128)(2,1)S(1)} %get-tuple-element.11.refs_1_, bf16[8,128,128]{2,1,0:T(8,128)(2,1)S(1)} %copy-done.1, ...), custom_call_target="tpu_custom_call" | custom-call | tf_op jit(solution)/shard_map/pallas_call | solution.py:431
  53.2 0.6 %copy.16 = bf16[8,16,256]{2,1,0:T(8,128)(2,1)} copy(bf16[8,16,256]{2,1,0:T(8,128)(2,1)S(1)} %get-tuple-element.20) | data formatting | bytes 131072
  53.9 0.7 %copy.17 = bf16[4,128,128]{2,1,0:T(8,128)(2,1)} copy(bf16[4,128,128]{2,1,0:T(8,128)(2,1)S(1)} %get-tuple-element.21) | data formatting | bytes 262144
  54.5 0.7 %copy.18 = f32[128,256]{1,0:T(8,128)} copy(f32[128,256]{1,0:T(8,128)S(1)} %get-tuple-element.22) | data formatting | bytes 262144
  55.2 0.8 %copy.19 = f32[3,3,128,128]{3,2,1,0:T(8,128)} copy(f32[3,3,128,128]{3,2,1,0:T(8,128)S(1)} %bitcast.5) | data formatting | bytes 1179648
Async XLA Ops:
  0.6 1.7 %copy-start.4 = (bf16[8,256,256]{2,1,0:T(8,128)(2,1)S(1)}, bf16[8,256,256]{2,1,0:T(8,128)(2,1)}, u32[]{:S(2)}) copy-start(bf16[8,256,256]{2,1,0:T(8,128)(2,1)} %tf_ref.1) | copy-start | bytes 3145732
  0.6 1.7 %copy-start.1 = (bf16[8,128,128]{2,1,0:T(8,128)(2,1)S(1)}, bf16[8,128,128]{2,1,0:T(8,128)(2,1)}, u32[]{:S(2)}) copy-start(bf16[8,128,128]{2,1,0:T(8,128)(2,1)} %refs_2_.1) | copy-start | bytes 786436
  0.7 1.7 %copy-start.3 = (bf16[128,256]{1,0:T(8,128)(2,1)S(1)}, bf16[128,256]{1,0:T(8,128)(2,1)}, u32[]{:S(2)}) copy-start(bf16[128,256]{1,0:T(8,128)(2,1)} %refs_4_.1) | copy-start | bytes 196612
  0.7 1.7 %copy-start.5 = (s32[2,8,128]{2,1,0:T(8,128)S(1)}, s32[2,8,128]{2,1,0:T(8,128)}, u32[]{:S(2)}) copy-start(s32[2,8,128]{2,1,0:T(8,128)} %cen_ref.1) | copy-start | bytes 24580
  2.4 16.9 %copy-start = (bf16[3,3,128,128]{3,2,1,0:T(8,128)(2,1)S(1)}, bf16[3,3,128,128]{3,2,1,0:T(8,128)(2,1)}, u32[]{:S(2)}) copy-start(bf16[3,3,128,128]{3,2,1,0:T(8,128)(2,1)} %refs_5_.1) | copy-start | bytes 884740
  2.4 16.9 %copy-start.2 = (bf16[4,128,128]{2,1,0:T(8,128)(2,1)S(1)}, bf16[4,128,128]{2,1,0:T(8,128)(2,1)}, u32[]{:S(2)}) copy-start(bf16[4,128,128]{2,1,0:T(8,128)(2,1)} %refs_3_.1) | copy-start | bytes 393220
